TPU v7x, 32 devices: a whole 2x2x4 slice. The times are simulated.
32 devices in a mesh: pipe: 4 (over z), dp: 8 (over y, x, core).
Axes of the slice: x: 2, y: 2, z: 4, core: 2. Of those that a mesh axis runs over, the one named last changes fastest.
Arguments:
- section_input: bfloat16 [4, 1024, 4096], P('pipe', 'dp'), may hold values from -6 to 6
- out_grad: bfloat16 [4, 1024, 4096], P('pipe', 'dp'), may hold values from -6 to 6
- short_filter: bfloat16 [4, 2, 7, 4096], P('pipe', None, None, 'dp'), may hold values from -2 to 2
- long_filter: bfloat16 [4, 2, 256, 128], P('pipe', None, 'dp'), may hold values from -0.5 to 0.5
Outputs:
- passed_grad: bfloat16 [4, 1024, 4096], P('pipe', 'dp')
- short_grad: float32 [4, 2, 7, 4096], P('pipe', None, None, 'dp')
- long_grad: float32 [4, 2, 256, 128], P('pipe', None, 'dp')
All inputs are finite; a program needn't handle non-finite values.
Results may differ from a plain program's by a relative error of at most 0.0058.
Values may be sent and summed in bfloat16 or wider, within the bound.
A program may use at most 64 MiB of HBM per device.

v0:
```python
import jax
import jax.numpy as jnp
from jax import lax
from jax.sharding import PartitionSpec as P


def from_behind(shard, axis, by):
    devices = lax.axis_size(axis)
    pairs = [(i, i + by) for i in range(devices) if 0 <= i + by < devices]
    return lax.ppermute(shard, axis, pairs)


def circulants(long_pair):
    pair_count, group_count, taps = long_pair.shape
    row_pos = jnp.arange(taps, dtype=jnp.int32)[:, None]
    col_pos = jnp.arange(taps, dtype=jnp.int32)[None, :]
    lag_table = (col_pos - row_pos + taps) % taps
    table = (lag_table.reshape(1, -1) == jnp.arange(taps, dtype=jnp.int32)[:, None]).astype(
        jnp.bfloat16
    )
    flat = jnp.dot(long_pair.reshape(-1, taps), table, preferred_element_type=jnp.float32).astype(
        jnp.bfloat16
    )
    circ = flat.reshape(pair_count, group_count, taps, taps)
    upper = row_pos <= col_pos
    zero_value = jnp.zeros((), jnp.bfloat16)
    return (jnp.where(upper, circ, zero_value), jnp.where(upper, zero_value, circ))


def as_groups(field, group_count, taps):
    return field.reshape(group_count, field.shape[0] // group_count, field.shape[1] // taps, taps)


def causal_long(field, circ_now, circ_past):
    group_count, taps = (circ_now.shape[0], circ_now.shape[2])
    blocks = as_groups(field, group_count, taps)
    earlier_blocks = jnp.concatenate([jnp.zeros_like(blocks[:, :, :1]), blocks[:, :, :-1]], axis=2)
    total = jnp.einsum("gcbt,gts->gcbs", blocks, circ_now, preferred_element_type=jnp.float32)
    total = total + jnp.einsum(
        "gcbt,gts->gcbs", earlier_blocks, circ_past, preferred_element_type=jnp.float32
    )
    return total.reshape(field.shape)


def anti_long(grad, circ_now, circ_past):
    group_count, taps = (circ_now.shape[0], circ_now.shape[2])
    blocks = as_groups(grad, group_count, taps)
    later_blocks = jnp.concatenate([blocks[:, :, 1:], jnp.zeros_like(blocks[:, :, :1])], axis=2)
    total = jnp.einsum("gcbs,gts->gcbt", blocks, circ_now, preferred_element_type=jnp.float32)
    total = total + jnp.einsum(
        "gcbs,gts->gcbt", later_blocks, circ_past, preferred_element_type=jnp.float32
    )
    return total.reshape(grad.shape)


def lag_grad(values, grad, group_count, taps):
    value_blocks = as_groups(values, group_count, taps)
    grad_blocks = as_groups(grad, group_count, taps)
    earlier_blocks = jnp.concatenate(
        [jnp.zeros_like(value_blocks[:, :, :1]), value_blocks[:, :, :-1]], axis=2
    )
    pairs_now = jnp.einsum(
        "gcbt,gcbs->gts", value_blocks, grad_blocks, preferred_element_type=jnp.float32
    )
    pairs_past = jnp.einsum(
        "gcbt,gcbs->gts", earlier_blocks, grad_blocks, preferred_element_type=jnp.float32
    )
    row_pos = jnp.arange(taps, dtype=jnp.int32)[:, None]
    col_pos = jnp.arange(taps, dtype=jnp.int32)[None, :]
    joined = jnp.where(row_pos <= col_pos, pairs_now, pairs_past)
    doubled = jnp.concatenate([joined, joined], axis=2).reshape(group_count, 2 * taps * taps)
    padded = jnp.concatenate([doubled, jnp.zeros((group_count, taps), jnp.float32)], axis=1)
    skewed = padded.reshape(group_count, taps, 2 * taps + 1)[:, :, :taps]
    return jnp.sum(skewed, axis=1)


def short_mix(field, taps_row):
    tap_count = taps_row.shape[0]
    extra = tap_count - 1
    row_count = field.shape[1]
    padded = jnp.concatenate([jnp.zeros((field.shape[0], extra), field.dtype), field], axis=1)
    total = jnp.zeros(field.shape, jnp.float32)
    for tap_index in range(tap_count):
        start = extra - tap_index
        total = total + taps_row[tap_index].astype(jnp.float32)[:, None] * padded[
            :, start : start + row_count
        ].astype(jnp.float32)
    return total


def short_back(field, taps_row):
    tap_count = taps_row.shape[0]
    extra = tap_count - 1
    row_count = field.shape[1]
    padded = jnp.concatenate([field, jnp.zeros((field.shape[0], extra), field.dtype)], axis=1)
    total = jnp.zeros(field.shape, jnp.float32)
    for tap_index in range(tap_count):
        total = total + taps_row[tap_index].astype(jnp.float32)[:, None] * padded[
            :, tap_index : tap_index + row_count
        ].astype(jnp.float32)
    return total


def short_corr(grad, field, tap_count):
    extra = tap_count - 1
    row_count = field.shape[1]
    padded = jnp.concatenate([jnp.zeros((field.shape[0], extra), field.dtype), field], axis=1)
    grad_wide = grad.astype(jnp.float32)
    rows_out = []
    for tap_index in range(tap_count):
        start = extra - tap_index
        rows_out.append(
            jnp.sum(grad_wide * padded[:, start : start + row_count].astype(jnp.float32), axis=1)
        )
    return jnp.stack(rows_out)


def body(section_input, out_grad, short_filter, long_filter):
    input_rows, grad_rows = (
        lax.all_to_all(section_input[0], "dp", split_axis=1, concat_axis=0, tiled=True),
        lax.all_to_all(out_grad[0], "dp", split_axis=1, concat_axis=0, tiled=True),
    )
    source = input_rows.T
    top_grad = grad_rows.T
    short_all = short_filter[0]
    long_all = long_filter[0]
    group_count, taps = (long_all.shape[1], long_all.shape[2])
    tap_count = short_all.shape[1]
    circ_now, circ_past = circulants(long_all)
    mixed_one = short_mix(source, short_all[0]).astype(jnp.bfloat16)
    long_one = causal_long(mixed_one, circ_now[0], circ_past[0])
    middle = (source.astype(jnp.float32) + long_one).astype(jnp.bfloat16)
    mixed_two = short_mix(middle, short_all[1]).astype(jnp.bfloat16)
    dmix_two = anti_long(top_grad, circ_now[1], circ_past[1]).astype(jnp.bfloat16)
    dlong_two = lag_grad(mixed_two, top_grad, group_count, taps)
    middle_grad = (top_grad.astype(jnp.float32) + short_back(dmix_two, short_all[1])).astype(
        jnp.bfloat16
    )
    dshort_two = short_corr(dmix_two, middle, tap_count)
    dmix_one = anti_long(middle_grad, circ_now[0], circ_past[0]).astype(jnp.bfloat16)
    dlong_one = lag_grad(mixed_one, middle_grad, group_count, taps)
    input_grad = (middle_grad.astype(jnp.float32) + short_back(dmix_one, short_all[0])).astype(
        jnp.bfloat16
    )
    dshort_one = short_corr(dmix_one, source, tap_count)
    flipped = input_grad.T
    own_rows = lax.all_to_all(flipped, "dp", split_axis=0, concat_axis=1, tiled=True)
    passed_grad = from_behind(own_rows, "pipe", -1)[None]
    factor = float(source.shape[1]) ** (-0.5)
    short_grad = jnp.stack([dshort_one, dshort_two])[None] * factor
    long_grad = jnp.stack([dlong_one, dlong_two])[None] * factor
    return (passed_grad, short_grad, long_grad)


def solution(mesh):
    in_specs = (
        P("pipe", "dp", None),
        P("pipe", "dp", None),
        P("pipe", None, None, "dp"),
        P("pipe", None, "dp", None),
    )
    out_specs = (P("pipe", "dp", None), P("pipe", None, None, "dp"), P("pipe", None, "dp", None))
    return jax.shard_map(body, mesh=mesh, in_specs=in_specs, out_specs=out_specs, check_vma=False)
```

profile of v0, /device:TPU:13, one launch (start us, length us, event | category | flops | bytes accessed | tf_op | source)
XLA Modules:
  0.0 133.2 jit_solution(5910072450399302204)
XLA Ops:
  0.7 2.4 %copy.35 = bf16[1,128,4096]{1,2,0:T(8,128)(2,1)} copy(bf16[1,128,4096]{2,1,0:T(8,128)(2,1)} %param.5) | data formatting | bytes 2097152 | tf_op args[1]
  3.0 5.0 %all-to-all-start = ((bf16[128,8,512]{0,2,1:T(8,128)(2,1)}), bf16[128,8,512]{0,2,1:T(8,128)(2,1)}, u32[]{:S(2)}, u32[]{:S(2)}) async-start(bf16[128,8,512]{0,2,1:T(8,128)(2,1)} %bitcast), calls=%async_computation | async-start | bytes 2097152 | tf_op jit(solution)/shard_map/all_to_all | solution.py:121
  9.5 2.0 %fusion.47 = bf16[8,8,128,128]{3,1,2,0:T(8,128)(2,1)S(1)} fusion(bf16[64,128]{1,0:T(8,128)(2,1)S(1)} %bitcast.226, s32[16384]{0:T(1024)S(1)} %add_select_fusion), kind=kOutput, calls=%fused_computation.90 | convolution fusion | flops 271581184 | bytes 2179072 | tf_op jit(solution)/shard_map/dot_general | solution.py:21
  12.2 1.6 %bitcast_select_fusion = (bf16[2,32,128,128]{3,2,1,0:T(8,128)(2,1)S(1)}, bf16[2,32,128,128]{3,2,1,0:T(8,128)(2,1)}) fusion(pred[128,128]{1,0:T(8,128)(4,1)S(1)} %iota_compare_fusion.4, bf16[2,32,128,128]{3,2,1,0:T(8,128)(2,1)S(1)} %bitcast.250), kind=kLoop, calls=%fused_computation.81 | loop fusion | flops 2097152 | bytes 6307840 | tf_op jit(solution)/shard_map/jit(_where)/select_n | solution.py:27
  13.8 5.8 %all-to-all-done = bf16[128,8,512]{0,2,1:T(8,128)(2,1)} async-done(((bf16[128,8,512]{0,2,1:T(8,128)(2,1)}), bf16[128,8,512]{0,2,1:T(8,128)(2,1)}, u32[]{:S(2)}, u32[]{:S(2)}) %all-to-all-start) | async-done | bytes 1048608 | tf_op jit(solution)/shard_map/all_to_all | solution.py:121
  19.7 8.0 %all-to-all-start.2 = ((bf16[128,8,512]{0,2,1:T(8,128)(2,1)}), bf16[128,8,512]{0,2,1:T(8,128)(2,1)}, u32[]{:S(2)}, u32[]{:S(2)}) async-start(bf16[128,8,512]{0,2,1:T(8,128)(2,1)} %bitcast.37), calls=%async_computation.2 | async-start | bytes 2097152 | tf_op jit(solution)/shard_map/all_to_all | solution.py:120
  27.6 1.5 %bitcast_bitcast_fusion.1 = bf16[64,8,8,128]{3,1,2,0:T(8,128)(2,1)S(1)} fusion(bf16[128,8,512]{0,2,1:T(8,128)(2,1)} %all-to-all-done), kind=kLoop, calls=%fused_computation.95 | loop fusion | bytes 2097152
  33.0 4.5 %fusion.23 = bf16[512,1024]{1,0:T(8,128)(2,1)S(1)} fusion(bf16[512,1024]{1,0:T(8,128)(2,1)S(1)} %bitcast.253, f32[512]{0:T(512)S(1)} %bitcast.259, f32[512]{0:T(512)S(1)} %bitcast.261, f32[512]{0:T(512)S(1)} %bitcast.263, f32[512]{0:T(512)S(1)} %bitcast.265, f32[512]{0:T(512)S(1)} %bitcast.267, f32[512]{0:T(512)S(1)} %bitcast.269, f32[512]{0:T(512)S(1)} %bitcast.271, ...), kind=kLoop, calls=%fused_computation.58 | loop fusion | flops 12058624 | bytes 3160064 | tf_op jit(solution)/shard_map/convert_element_type | solution.py:136
  40.9 1.4 %copy.124 = bf16[64,8,8,128]{3,1,2,0:T(8,128)(2,1)} copy(bf16[64,8,8,128]{3,2,1,0:T(8,128)(2,1)S(1)} %bitcast.243) | data formatting | bytes 2097152
  42.4 1.5 %bitcast_bitcast_fusion = bf16[512,1024]{1,0:T(8,128)(2,1)S(1)} fusion(bf16[128,8,512]{0,2,1:T(8,128)(2,1)} %all-to-all-done.2), kind=kLoop, calls=%fused_computation.94 | loop fusion | bytes 2097152 | tf_op jit(solution)/shard_map/transpose | solution.py:123
  44.2 6.1 %fusion.51 = (bf16[64,8,8,128]{3,1,2,0:T(8,128)(2,1)S(1)}, bf16[64,8,8,128]{3,2,1,0:T(8,128)(2,1)}) fusion(f32[512]{0:T(512)S(1)} %bitcast.285, f32[512]{0:T(512)S(1)} %bitcast.286, f32[512]{0:T(512)S(1)} %bitcast.281, f32[512]{0:T(512)S(1)} %bitcast.282, f32[512]{0:T(512)S(1)} %bitcast.283, f32[512]{0:T(512)S(1)} %bitcast.284, ...), kind=kLoop, calls=%fused_computation.113 | loop fusion | flops 23068672 | bytes 5257216
  50.6 1.3 copy-done.6
  54.8 4.6 %fusion.45 = (f32[512]{0:T(512)S(1)}, f32[512]{0:T(512)S(1)}, f32[512]{0:T(512)S(1)}, f32[512]{0:T(512)S(1)}, f32[512]{0:T(512)S(1)}, /*index=5*/f32[512]{0:T(512)S(1)}, f32[512]{0:T(512)S(1)}, bf16[512,1024]{1,0:T(8,128)(2,1)S(1)}) fusion(bf16[512,1024]{1,0:T(8,128)(2,1)S(1)} %bitcast_bitcast_fusion, bf16[64,8,8,128]{3,2,1,0:T(8,128)(2,1)S(1)} %bitcast.244, ...), kind=kLoop, calls=%fused_computation.80 | loop fusion | flops 12579328 | bytes 6305792 | tf_op jit(solution)/shard_map/reduce_sum | solution.py:113
  59.4 6.6 %fusion.30 = (f32[512]{0:T(512)S(1)}, f32[512]{0:T(512)S(1)}, f32[512]{0:T(512)S(1)}, f32[512]{0:T(512)S(1)}, f32[512]{0:T(512)S(1)}, /*index=5*/f32[512]{0:T(51...) fusion(bf16[512,1024]{1,0:T(8,128)(2,1)S(1)} %get-tuple-element.26, bf16[64,8,8,128]{3,2,1,0:T(8,128)(2,1)S(1)} %bitcast.246, ...), kind=kLoop, calls=%fused_computation.65 | loop fusion | flops 22016512 | bytes 3174400 | tf_op jit(solution)/shard_map/reduce_sum | solution.py:113
  66.7 2.5 %copy.73 = bf16[64,8,8,128]{3,2,1,0:T(8,128)(2,1)} copy(bf16[64,8,8,128]{3,1,2,0:T(8,128)(2,1)} %get-tuple-element.25) | data formatting | bytes 2097152
  70.3 5.0 %all-to-all-start.1 = ((bf16[8,128,512]{1,2,0:T(8,128)(2,1)}), bf16[8,128,512]{1,2,0:T(8,128)(2,1)}, u32[]{:S(2)}, u32[]{:S(2)}) async-start(bf16[8,128,512]{1,2,0:T(8,128)(2,1)} %bitcast.252), calls=%async_computation.1 | async-start | bytes 2097152 | tf_op jit(solution)/shard_map/all_to_all | solution.py:147
  75.3 1.8 %fusion.62 = f32[32,128,128,1]{1,2,3,0:T(8,128)S(1)} fusion(bf16[32,16,8,128]{3,2,1,0:T(8,128)(2,1)} %bitcast.248, bf16[32,16,8,128]{3,2,1,0:T(8,128)(2,1)S(1)} %bitcast.233), kind=kOutput, calls=%fused_computation.154 | convolution fusion | flops 134217728 | bytes 4194304 | tf_op jit(solution)/shard_map/gcbt,gcbs->gts/dot_general | solution.py:62
  77.7 2.4 %pad_maximum_fusion.1 = f32[32,128,256]{1,2,0:T(8,128)} fusion(f32[32,128,128]{1,2,0:T(8,128)S(1)} %bitcast_select_fusion.2), kind=kLoop, calls=%fused_computation.19 | loop fusion | flops 1048576 | bytes 6291456 | tf_op jit(solution)/shard_map/concatenate | solution.py:71
  80.2 5.4 %copy.74 = f32[4,8,128,256]{3,1,2,0:T(8,128)} copy(f32[4,8,128,256]{2,3,1,0:T(8,128)} %bitcast.240) | data formatting | bytes 8388608
  85.6 4.5 %concatenate.64 = f32[32,32896]{1,0:T(8,128)} pad(f32[32,32768]{1,0:T(8,128)} %bitcast.241, f32[]{:T(128)} %constant.24.clone.1), padding=0_0x0_128 | pad | bytes 8404996 | tf_op jit(solution)/shard_map/concatenate | solution.py:72
  90.1 8.0 %reshape.286 = f32[32,128,257]{2,1,0:T(8,128)} reshape(f32[32,32896]{1,0:T(8,128)} %concatenate.64) | data formatting | bytes 8421376 | tf_op jit(solution)/shard_map/reshape | solution.py:73
  98.1 1.9 %fusion.64 = f32[32,128,128,1]{1,2,3,0:T(8,128)} fusion(bf16[32,16,8,128]{3,2,1,0:T(8,128)(2,1)S(1)} %bitcast.237, bf16[32,16,8,128]{3,2,1,0:T(8,128)(2,1)S(1)} %bitcast.229), kind=kOutput, calls=%fused_computation.156 | convolution fusion | flops 134217728 | bytes 4194304 | tf_op jit(solution)/shard_map/gcbt,gcbs->gts/dot_general | solution.py:62
  100.0 2.3 %copy.41 = bf16[128,4096]{1,0:T(8,128)(2,1)} copy(bf16[128,4096]{0,1:T(8,128)(2,1)} %bitcast.35) | data formatting | bytes 2097152 | tf_op jit(solution)/shard_map/all_to_all | solution.py:147
  102.2 1.9 %collective-permute-start = (bf16[128,4096]{1,0:T(8,128)(2,1)}, bf16[128,4096]{1,0:T(8,128)(2,1)}, u32[]{:S(2)}, u32[]{:S(2)}) collective-permute-start(bf16[128,4096]{1,0:T(8,128)(2,1)} %copy.41), channel_id=1, source_target_pairs={{8,0},{16,8},{24,16},{9,1},{17,9},{25,17},{10,2},{18,10},{26,18},{... | collective-permute-start | bytes 3145736 | tf_op jit(solution)/shard_map/ppermute | solution.py:10
  104.1 2.4 %bitcast_select_fusion.3 = f32[32,128,128]{1,2,0:T(8,128)S(1)} fusion(f32[32,128,128,1]{1,2,3,0:T(8,128)} %fusion.64, pred[128,128]{0,1:T(8,128)(4,1)S(1)} %copy.44, bf16[32,16,7,128]{3,2,1,0:T(8,128)(2,1)S(1)} %bitcast.238, bf16[32,16,8,128]{3,2,1,0:T(8,128)(2,1)S(1)} %bitcast.230), kind=kOutput, calls=%fused_computation.86 | convolution fusion | flops 134742016 | bytes 6176768 | tf_op jit(solution)/shard_map/gcbt,gcbs->gts/dot_general | solution.py:65
  106.5 2.6 %pad_maximum_fusion = f32[32,128,256]{1,2,0:T(8,128)} fusion(f32[32,128,128]{1,2,0:T(8,128)S(1)} %bitcast_select_fusion.3), kind=kLoop, calls=%fused_computation.18 | loop fusion | flops 1048576 | bytes 6291456 | tf_op jit(solution)/shard_map/concatenate | solution.py:71
  109.1 5.4 %copy.72 = f32[4,8,128,256]{3,1,2,0:T(8,128)} copy(f32[4,8,128,256]{2,3,1,0:T(8,128)} %bitcast.242) | data formatting | bytes 8388608
  114.5 4.4 %concatenate.61 = f32[32,32896]{1,0:T(8,128)} pad(f32[32,32768]{1,0:T(8,128)} %bitcast.239, f32[]{:T(128)} %constant.24.clone.1), padding=0_0x0_128 | pad | bytes 8404996 | tf_op jit(solution)/shard_map/concatenate | solution.py:72
  118.9 7.9 %reshape.283 = f32[32,128,257]{2,1,0:T(8,128)} reshape(f32[32,32896]{1,0:T(8,128)} %concatenate.61) | data formatting | bytes 8421376 | tf_op jit(solution)/shard_map/reshape | solution.py:73
  126.8 1.7 %slice_reduce_fusion = f32[32,128]{1,0:T(8,128)S(1)} fusion(f32[32,128,257]{2,1,0:T(8,128)} %reshape.286), kind=kLoop, calls=%fused_computation.83 | loop fusion | flops 520192 | bytes 2113536 | tf_op jit(solution)/shard_map/reduce_sum | solution.py:74
  128.6 1.7 %slice_reduce_fusion.1 = f32[32,128]{1,0:T(8,128)S(1)} fusion(f32[32,128,257]{2,1,0:T(8,128)} %reshape.283), kind=kLoop, calls=%fused_computation.84 | loop fusion | flops 520192 | bytes 2113536 | tf_op jit(solution)/shard_map/reduce_sum | solution.py:74
  130.9 2.3 %copy.128 = bf16[1,128,4096]{2,1,0:T(8,128)(2,1)} copy(bf16[1,128,4096]{2,1,0:T(8,128)(2,1)} %bitcast.36) | data formatting | bytes 2097152
  (64 shorter events, 15.8 us)
Async XLA Ops:
  0.6 8.8 %copy-start = (bf16[1,2,32,128]{3,2,1,0:T(8,128)(2,1)S(1)}, bf16[1,2,32,128]{3,2,1,0:T(8,128)(2,1)}, u32[]{:S(2)}) copy-start(bf16[1,2,32,128]{3,2,1,0:T(8,128)(2,1)} %param.7) | copy-start | bytes 49156
  0.6 7.5 %copy-start.16 = (bf16[1,128,4096]{2,1,0:T(8,128)(2,1)S(1)}, bf16[1,128,4096]{2,1,0:T(8,128)(2,1)}, u32[]{:S(2)}) copy-start(bf16[1,128,4096]{2,1,0:T(8,128)(2,1)} %param.4) | copy-start | bytes 3145732
  3.0 16.6 %all-to-all-start = ((bf16[128,8,512]{0,2,1:T(8,128)(2,1)}), bf16[128,8,512]{0,2,1:T(8,128)(2,1)}, u32[]{:S(2)}, u32[]{:S(2)}) async-start(bf16[128,8,512]{0,2,1:T(8,128)(2,1)} %bitcast), calls=%async_computation | async-start | bytes 2097152 | tf_op jit(solution)/shard_map/all_to_all | solution.py:121
  11.5 0.7 copy-start.17
  13.8 17.8 %copy-start.2 = (bf16[2,32,128,128]{3,2,1,0:T(8,128)(2,1)}, bf16[2,32,128,128]{3,2,1,0:T(8,128)(2,1)S(1)}, u32[]{:S(2)}) copy-start(bf16[2,32,128,128]{3,2,1,0:T(8,128)(2,1)S(1)} %get-tuple-element.23) | copy-start | bytes 6291460
  19.7 22.7 %all-to-all-start.2 = ((bf16[128,8,512]{0,2,1:T(8,128)(2,1)}), bf16[128,8,512]{0,2,1:T(8,128)(2,1)}, u32[]{:S(2)}, u32[]{:S(2)}) async-start(bf16[128,8,512]{0,2,1:T(8,128)(2,1)} %bitcast.37), calls=%async_computation.2 | async-start | bytes 2097152 | tf_op jit(solution)/shard_map/all_to_all | solution.py:120
  29.2 1.6 %copy-start.5 = (bf16[2,32,128,128]{3,2,1,0:T(8,128)(2,1)S(1)}, bf16[2,32,128,128]{3,2,1,0:T(8,128)(2,1)}, u32[]{:S(2)}) copy-start(bf16[2,32,128,128]{3,2,1,0:T(8,128)(2,1)} %get-tuple-element.24) | copy-start | bytes 6291460
  32.8 4.8 %copy-start.9 = (bf16[32,16,8,128]{3,2,1,0:T(8,128)(2,1)}, bf16[32,16,8,128]{3,2,1,0:T(8,128)(2,1)S(1)}, u32[]{:S(2)}) copy-start(bf16[32,16,8,128]{3,2,1,0:T(8,128)(2,1)S(1)} %copy.39) | copy-start | bytes 3145732
  37.5 1.0 copy-start.11
  38.5 1.6 %copy-start.3 = (bf16[2,32,128,128]{3,2,1,0:T(8,128)(2,1)S(1)}, bf16[2,32,128,128]{3,2,1,0:T(8,128)(2,1)}, u32[]{:S(2)}) copy-start(bf16[2,32,128,128]{3,2,1,0:T(8,128)(2,1)} %copy-done.2) | copy-start | bytes 6291460
  40.9 3.0 %copy-start.7 = (bf16[32,16,8,128]{3,2,1,0:T(8,128)(2,1)}, bf16[32,16,8,128]{3,2,1,0:T(8,128)(2,1)S(1)}, u32[]{:S(2)}) copy-start(bf16[32,16,8,128]{3,2,1,0:T(8,128)(2,1)S(1)} %add_convert_fusion) | copy-start | bytes 3145732
  42.4 1.5 %copy-start.12 = (bf16[512,1024]{1,0:T(8,128)(2,1)S(1)}, bf16[512,1024]{1,0:T(8,128)(2,1)}, u32[]{:S(2)}) copy-start(bf16[512,1024]{1,0:T(8,128)(2,1)} %copy-done.11) | copy-start | bytes 3145732
  42.4 1.9 %copy-start.15 = (bf16[64,8,8,128]{3,1,2,0:T(8,128)(2,1)S(1)}, bf16[64,8,8,128]{3,1,2,0:T(8,128)(2,1)}, u32[]{:S(2)}) copy-start(bf16[64,8,8,128]{3,1,2,0:T(8,128)(2,1)} %copy.124) | copy-start | bytes 3145732
  50.4 1.6 %copy-start.6 = (bf16[2,32,128,128]{3,2,1,0:T(8,128)(2,1)S(1)}, bf16[2,32,128,128]{3,2,1,0:T(8,128)(2,1)}, u32[]{:S(2)}) copy-start(bf16[2,32,128,128]{3,2,1,0:T(8,128)(2,1)} %get-tuple-element.24) | copy-start | bytes 6291460
  51.9 1.6 %copy-start.4 = (bf16[2,32,128,128]{3,2,1,0:T(8,128)(2,1)S(1)}, bf16[2,32,128,128]{3,2,1,0:T(8,128)(2,1)}, u32[]{:S(2)}) copy-start(bf16[2,32,128,128]{3,2,1,0:T(8,128)(2,1)} %copy-done.2) | copy-start | bytes 6291460
  53.5 1.2 copy-start.8
  54.8 4.6 %copy-start.10 = (bf16[32,16,8,128]{3,2,1,0:T(8,128)(2,1)S(1)}, bf16[32,16,8,128]{3,2,1,0:T(8,128)(2,1)}, u32[]{:S(2)}) copy-start(bf16[32,16,8,128]{3,2,1,0:T(8,128)(2,1)} %copy-done.9) | copy-start | bytes 3145732
  66.0 3.2 %copy-start.14 = (bf16[64,8,8,128]{3,2,1,0:T(8,128)(2,1)S(1)}, bf16[64,8,8,128]{3,2,1,0:T(8,128)(2,1)}, u32[]{:S(2)}) copy-start(bf16[64,8,8,128]{3,2,1,0:T(8,128)(2,1)} %get-tuple-element.28) | copy-start | bytes 3145732
  70.3 29.6 %all-to-all-start.1 = ((bf16[8,128,512]{1,2,0:T(8,128)(2,1)}), bf16[8,128,512]{1,2,0:T(8,128)(2,1)}, u32[]{:S(2)}, u32[]{:S(2)}) async-start(bf16[8,128,512]{1,2,0:T(8,128)(2,1)} %bitcast.252), calls=%async_computation.1 | async-start | bytes 2097152 | tf_op jit(solution)/shard_map/all_to_all | solution.py:147
  75.3 1.8 %copy-start.13 = (bf16[64,8,8,128]{3,2,1,0:T(8,128)(2,1)S(1)}, bf16[64,8,8,128]{3,2,1,0:T(8,128)(2,1)}, u32[]{:S(2)}) copy-start(bf16[64,8,8,128]{3,2,1,0:T(8,128)(2,1)} %copy.73) | copy-start | bytes 3145732
  102.2 28.7 %collective-permute-start = (bf16[128,4096]{1,0:T(8,128)(2,1)}, bf16[128,4096]{1,0:T(8,128)(2,1)}, u32[]{:S(2)}, u32[]{:S(2)}) collective-permute-start(bf16[128,4096]{1,0:T(8,128)(2,1)} %copy.41), channel_id=1, source_target_pairs={{8,0},{16,8},{24,16},{9,1},{17,9},{25,17},{10,2},{18,10},{26,18},{... | collective-permute-start | bytes 3145736 | tf_op jit(solution)/shard_map/ppermute | solution.py:10
  126.8 6.4 %copy-start.1 = (bf16[1,2,32,128]{3,2,1,0:T(8,128)(2,1)S(1)}, bf16[1,2,32,128]{3,2,1,0:T(8,128)(2,1)}, u32[]{:S(2)}) copy-start(bf16[1,2,32,128]{3,2,1,0:T(8,128)(2,1)} %param.7) | copy-start | bytes 49156
where the time goes:
time: 136 us; the launch traced here: 133 us
  local copies, waits for them, and re-layouts  61.1 us (45%)
  other arithmetic  32.5 us (24%)
  starting transfers between devices  19.8 us (15%)
  matrix products  12.9 us (9%)
  waiting for transfers between devices  5.84 us (4%)
    unnamed x50, local copies, waits for them, and re-layouts  30.3 us
    reshape x2, local copies, waits for them, and re-layouts, lag_grad(): skewed = padded.reshape(group_count, taps, 2 * taps + 1)[:, :, :taps]  15.9 us
    reduce_sum x2, other arithmetic, short_corr(): jnp.sum(grad_wide * padded[:, start:start + row_count].astype(jnp.float32...  11.2 us
    concatenate x2, local copies, waits for them, and re-layouts, lag_grad(): jnp.concatenate([doubled, jnp.zeros((group_count, taps), jnp.float32)], a...  8.91 us
    all_to_all x1, starting transfers between devices, body(): lax.all_to_all(section_input[0], 'dp', split_axis=1, concat_axis=0, tiled...  8 us
    unnamed x1, other arithmetic  6.13 us
    all_to_all x1, waiting for transfers between devices, body(): lax.all_to_all(out_grad[0], 'dp', split_axis=1, concat_axis=0, tiled=True)  5.83 us
    concatenate x2, other arithmetic, lag_grad(): jnp.concatenate([joined, joined], axis=2)  4.99 us
  transfers between devices with their start and end apart: 4, of which 1 were waited for; matrix products, arithmetic and copies ran while one was open for 52% of the time, Pallas kernels for 0%

commit v1 on v0

v1 whole, which is shorter than its diff:
```python
import functools

import jax
import jax.numpy as jnp
from jax import lax
from jax.experimental import pallas as pl
from jax.experimental.pallas import tpu as pltpu
from jax.sharding import PartitionSpec as P

MESH = pl.DeviceIdType.MESH
LANES = 128
PER_GROUP = 16
F32 = jnp.float32
BF16 = jnp.bfloat16
NT = (((1,), (1,)), ((), ()))
NN = (((1,), (0,)), ((), ()))
TN = (((0,), (0,)), ((), ()))


def mm(a, b, dims):
    return lax.dot_general(a, b, dims, preferred_element_type=F32)


def lanes_of(rows):
    return lax.broadcasted_iota(jnp.int32, (rows, LANES), 1)


def past_block(x):
    return jnp.concatenate([jnp.zeros((PER_GROUP, LANES), x.dtype), x[:-PER_GROUP]], axis=0)


def next_block(x):
    return jnp.concatenate([x[PER_GROUP:], jnp.zeros((PER_GROUP, LANES), x.dtype)], axis=0)


def shift_past(x, k):
    if k == 0:
        return x
    rolled = pltpu.roll(x, k, 1)
    return jnp.where(lanes_of(x.shape[0]) < k, past_block(rolled), rolled)


def shift_next(x, k):
    if k == 0:
        return x
    rolled = pltpu.roll(x, LANES - k, 1)
    return jnp.where(lanes_of(x.shape[0]) < LANES - k, rolled, next_block(rolled))


def kernel(n, pipes, chunks, tap_count, batch, factor,
           x_ref, g_ref, sf_ref, lf_ref,
           out_ref, short_ref, long_ref,
           recv, xt, ot, obuf, zbuf, wide, now_ref, past_ref, corr, lag,
           send_sem, recv_sem, local_sem, osend_sem, orecv_sem, zero_sem):
    stage = lax.axis_index("pipe")
    me = lax.axis_index("dp")
    rows = x_ref.shape[0]
    width = chunks * LANES
    per_chunk = LANES // PER_GROUP
    groups = chunks * per_chunk

    barrier = pltpu.get_barrier_semaphore()
    for j in range(1, n):
        pl.semaphore_signal(barrier, inc=1, device_id=(stage, lax.rem(me + j, n)), device_id_type=MESH)

    @pl.when(stage < pipes - 1)
    def _():
        for j in range(n):
            pl.semaphore_signal(barrier, inc=1, device_id=(stage + 1, j), device_id_type=MESH)

    pl.semaphore_wait(barrier, n - 1 + n * jnp.minimum(stage, 1))

    def columns(device, q):
        return pl.ds(pl.multiple_of(device * width + q * LANES, LANES), LANES)

    def in_copy(a, q, j, slot):
        to = lax.rem(me + j, n)
        return pltpu.make_async_remote_copy(
            src_ref=(x_ref, g_ref)[a].at[:, columns(to, q)],
            dst_ref=recv.at[a, q, slot],
            send_sem=send_sem.at[a, q, j],
            recv_sem=recv_sem.at[a, q, j],
            device_id=(stage, to),
            device_id_type=MESH,
        )

    def own_copy(a, q):
        return pltpu.make_async_copy(
            (x_ref, g_ref)[a].at[:, columns(me, q)], recv.at[a, q, me], local_sem.at[a, q]
        )

    def out_copy(q, j, source):
        to = lax.rem(me + j, n)
        return pltpu.make_async_remote_copy(
            src_ref=obuf.at[q, to],
            dst_ref=out_ref.at[:, columns(source, q)],
            send_sem=osend_sem.at[q, j],
            recv_sem=orecv_sem.at[q, j],
            device_id=(stage - 1, to),
            device_id_type=MESH,
        )

    @pl.loop(0, chunks)
    def _(q):
        for j in range(1, n):
            for a in range(2):
                in_copy(a, q, j, me).start()
        for a in range(2):
            own_copy(a, q).start()

    zero_copy = pltpu.make_async_copy(zbuf, out_ref, zero_sem)

    @pl.when(stage == pipes - 1)
    def _():
        zbuf[...] = jnp.zeros_like(zbuf)
        zero_copy.start()

    square = (LANES, LANES)
    row_pos = lax.broadcasted_iota(jnp.int32, square, 0)
    col_pos = lax.broadcasted_iota(jnp.int32, square, 1)
    eye = (row_pos == col_pos).astype(BF16)
    upper = row_pos <= col_pos

    @pl.loop(0, chunks)
    def _(q):
        for blk in range(2):
            taps_q = sf_ref[blk, :, pl.ds(pl.multiple_of(q * LANES, LANES), LANES)]
            for k in range(tap_count):
                spread = jnp.broadcast_to(taps_q[k:k + 1].astype(F32), square).astype(BF16)
                wide[q, blk * tap_count + k] = mm(eye, spread, NT)

    @pl.loop(0, groups)
    def _(g):
        for blk in range(2):
            filt = lf_ref[blk, pl.ds(g, 1)]
            circ = pltpu.roll(jnp.broadcast_to(filt, square), 0, 1, stride=1, stride_axis=0)
            now_ref[blk, g] = jnp.where(upper, circ, 0.0).astype(BF16)
            past_ref[blk, g] = jnp.where(upper, 0.0, circ).astype(BF16)

    def causal(v, blk, g):
        return mm(
            jnp.concatenate([v, past_block(v)], axis=1),
            jnp.concatenate([now_ref[blk, g], past_ref[blk, g]], axis=0), NN,
        )

    def anti(v, blk, g):
        return mm(
            jnp.concatenate([v, next_block(v)], axis=1),
            jnp.concatenate([now_ref[blk, g], past_ref[blk, g]], axis=1), NT,
        )

    def lag_part(values, grad, blk, g):
        pairs = mm(values, jnp.concatenate([grad, next_block(grad)], axis=1), TN)
        joined = jnp.where(upper, pairs[:, :LANES], pairs[:, LANES:])
        total = joined[:8]
        for i in range(1, LANES // 8):
            total = total + pltpu.roll(joined[8 * i:8 * i + 8], LANES - 8 * i, 1)
        lag[pl.ds(pl.multiple_of((blk * groups + g) * 8, 8), 8)] = total

    def tap(q, gl, blk, k):
        one = wide[q, blk * tap_count + k, pl.ds(pl.multiple_of(gl * PER_GROUP, PER_GROUP), PER_GROUP)]
        return jnp.concatenate([one] * n, axis=0)

    def short_mix(x, q, gl, blk):
        total = tap(q, gl, blk, 0) * x
        for k in range(1, tap_count):
            total = total + tap(q, gl, blk, k) * shift_past(x, k)
        return total.astype(BF16)

    def short_back(base, d, x, q, gl, blk):
        total = base
        at = pl.ds(pl.multiple_of(gl * PER_GROUP, PER_GROUP), PER_GROUP)
        for k in range(tap_count):
            moved = shift_next(d, k)
            total = total + tap(q, gl, blk, k) * moved
            prod = moved * x
            part = prod[:PER_GROUP]
            for b in range(1, n):
                part = part + prod[b * PER_GROUP:(b + 1) * PER_GROUP]
            corr[blk * tap_count + k, at] = part
        return total.astype(BF16)

    @pl.loop(0, chunks)
    def _(q):
        for j in range(1, n):
            for a in range(2):
                in_copy(a, q, j, lax.rem(me - j + n, n)).wait_recv()
        for a in range(2):
            own_copy(a, q).wait()
        for a in range(2):
            for b in range(n):
                turned = mm(eye, recv[a, q, b], NT).astype(BF16)
                xt[a, :, b * PER_GROUP:(b + 1) * PER_GROUP, :] = turned.reshape(
                    per_chunk, PER_GROUP, LANES
                )

        @pl.loop(0, per_chunk // batch)
        def _(step):
            local = [step * batch + u for u in range(batch)]
            every = range(batch)
            glob = [q * per_chunk + gl for gl in local]
            top = [xt[1, gl] for gl in local]
            src = [xt[0, gl].astype(F32) for gl in local]
            dmix_two = [anti(top[u], 1, glob[u]).astype(BF16).astype(F32) for u in every]
            mixed_one = [short_mix(src[u], q, local[u], 0) for u in every]
            long_one = [causal(mixed_one[u], 0, glob[u]) for u in every]
            middle = [(src[u] + long_one[u]).astype(BF16).astype(F32) for u in every]
            middle_grad = [
                short_back(top[u].astype(F32), dmix_two[u], middle[u], q, local[u], 1) for u in every
            ]
            dmix_one = [anti(middle_grad[u], 0, glob[u]).astype(BF16).astype(F32) for u in every]
            mixed_two = [short_mix(middle[u], q, local[u], 1) for u in every]
            for u in every:
                lag_part(mixed_two[u], top[u], 1, glob[u])
            for u in every:
                ot[local[u]] = short_back(
                    middle_grad[u].astype(F32), dmix_one[u], src[u], q, local[u], 0
                )
            for u in every:
                lag_part(mixed_one[u], middle_grad[u], 0, glob[u])

        @pl.when(stage > 0)
        def _():
            for b in range(n):
                piece = ot[:, b * PER_GROUP:(b + 1) * PER_GROUP, :].reshape(square)
                obuf[q, b] = mm(eye, piece, NT).astype(BF16)
            for j in range(n):
                out_copy(q, j, me).start()

        ones = jnp.ones((8, 2 * LANES), BF16)
        for blk in range(2):
            for k in range(tap_count):
                part = corr[blk * tap_count + k]
                high = part.astype(BF16)
                low = (part - high.astype(F32)).astype(BF16)
                summed = mm(ones, jnp.concatenate([high, low], axis=1), NT)
                short_ref[blk, k:k + 1, pl.ds(pl.multiple_of(q * LANES, LANES), LANES)] = (
                    summed[:1] * factor
                )

    total = lag[pl.ds(0, 2 * groups, stride=8), :]
    for r in range(1, 8):
        total = total + pltpu.roll(lag[pl.ds(r, 2 * groups, stride=8), :], LANES - r, 1)
    total = total * factor
    long_ref[0] = total[:groups]
    long_ref[1] = total[groups:]

    @pl.loop(0, chunks)
    def _(q):
        for j in range(1, n):
            for a in range(2):
                in_copy(a, q, j, me).wait_send()

    @pl.when(stage == pipes - 1)
    def _():
        zero_copy.wait()

    @pl.when(stage > 0)
    def _():
        @pl.loop(0, chunks)
        def _(q):
            for j in range(n):
                out_copy(q, j, me).wait_send()

    @pl.when(stage < pipes - 1)
    def _():
        @pl.loop(0, chunks)
        def _(q):
            for j in range(n):
                out_copy(q, j, lax.rem(me - j + n, n)).wait_recv()


def body(n, pipes, section_input, out_grad, short_filter, long_filter):
    rows, channels = section_input.shape[1:]
    tap_count = short_filter.shape[2]
    groups, taps = long_filter.shape[2:]
    width = channels // n
    chunks = width // LANES
    assert rows == LANES and taps == LANES and width == groups * PER_GROUP
    per_chunk = LANES // PER_GROUP
    batch = max(1, min(4, 32 // n))
    factor = float(rows * n) ** (-0.5)
    vmem = pl.BlockSpec(memory_space=pltpu.VMEM)
    anywhere = pl.BlockSpec(memory_space=pl.ANY)
    dma = pltpu.SemaphoreType.DMA
    passed, short_grad, long_grad = pl.pallas_call(
        functools.partial(kernel, n, pipes, chunks, tap_count, batch, factor),
        out_shape=(
            jax.ShapeDtypeStruct((rows, channels), BF16),
            jax.ShapeDtypeStruct((2, tap_count, width), F32),
            jax.ShapeDtypeStruct((2, groups, taps), F32),
        ),
        in_specs=[anywhere, anywhere, vmem, vmem],
        out_specs=(anywhere, vmem, vmem),
        scratch_shapes=[
            pltpu.VMEM((2, chunks, n, LANES, LANES), BF16),
            pltpu.VMEM((2, per_chunk, n * PER_GROUP, LANES), BF16),
            pltpu.VMEM((per_chunk, n * PER_GROUP, LANES), BF16),
            pltpu.VMEM((chunks, n, LANES, LANES), BF16),
            pltpu.VMEM((rows, channels), BF16),
            pltpu.VMEM((chunks, 2 * tap_count, LANES, LANES), F32),
            pltpu.VMEM((2, groups, LANES, LANES), BF16),
            pltpu.VMEM((2, groups, LANES, LANES), BF16),
            pltpu.VMEM((2 * tap_count, LANES, LANES), F32),
            pltpu.VMEM((2 * groups * 8, LANES), F32),
            dma((2, chunks, n)),
            dma((2, chunks, n)),
            dma((2, chunks)),
            dma((chunks, n)),
            dma((chunks, n)),
            dma(()),
        ],
        compiler_params=pltpu.CompilerParams(
            collective_id=0, has_side_effects=True, vmem_limit_bytes=48 * 1024 * 1024
        ),
    )(section_input[0], out_grad[0], short_filter[0], long_filter[0].astype(F32))
    return passed[None], short_grad[None], long_grad[None]


def solution(mesh):
    in_specs = (
        P("pipe", "dp", None),
        P("pipe", "dp", None),
        P("pipe", None, None, "dp"),
        P("pipe", None, "dp", None),
    )
    out_specs = (P("pipe", "dp", None), P("pipe", None, None, "dp"), P("pipe", None, "dp", None))
    run = functools.partial(body, mesh.shape["dp"], mesh.shape["pipe"])
    return jax.shard_map(run, mesh=mesh, in_specs=in_specs, out_specs=out_specs, check_vma=False)
```

time: 136 us -> 61.7 us (0.45); the launches traced: 133 us -> 61.4 us
  local copies, waits for them, and re-layouts: 61.1 us -> 5.39 us
  Pallas kernels: 0 us -> 55.4 us
  other arithmetic: 32.5 us -> 0.01 us
  starting transfers between devices: 19.8 us -> 0 us
  matrix products: 12.9 us -> 0 us
  waiting for transfers between devices: 5.84 us -> 0 us
    pallas_call x0 -> x1, Pallas kernels: none -> 55.4 us  [body(): pl.pallas_call(functools.partial(kernel, n, pipes, chunks, tap_count, bat...]
    unnamed x50 -> x10, local copies, waits for them, and re-layouts: 30.3 us -> 5.39 us
    all_to_all x3 -> x0, starting transfers between devices: 17.9 us -> none  [the longest x1 8 us: body(): lax.all_to_all(section_input[0], 'dp', split_axis=1, concat_axis=0, tiled...]
    reshape x2 -> x0, local copies, waits for them, and re-layouts: 15.9 us -> none  [lag_grad(): skewed = padded.reshape(group_count, taps, 2 * taps + 1)[:, :, :taps]]
    reduce_sum x4 -> x0, other arithmetic: 14.6 us -> none  [the longest x2 11.2 us: short_corr(): jnp.sum(grad_wide * padded[:, start:start + row_count].astype(jnp.float32...]
    dot_general x11 -> x0, matrix products: 12.9 us -> none  [the longest x2 3.71 us: lag_grad(): jnp.einsum('gcbt,gcbs->gts', value_blocks, grad_blocks, preferred_element...]
    concatenate x2 -> x0, local copies, waits for them, and re-layouts: 8.91 us -> none  [lag_grad(): jnp.concatenate([doubled, jnp.zeros((group_count, taps), jnp.float32)], a...]
    unnamed x1 -> x0, other arithmetic: 6.13 us -> none
  transfers between devices with their start and end apart: 4 -> 0, of which waited for: 1 -> 0; matrix products, arithmetic and copies ran while one was open for 52% -> 0% of each run, Pallas kernels for 0% -> 0%
where the time goes in v1:
time: 61.7 us; the launch traced here: 61.4 us
  Pallas kernels  55.4 us (90%)
  local copies, waits for them, and re-layouts  5.39 us (9%)
  between operations  0.66 us (1%)
    pallas_call x1, Pallas kernels, body(): pl.pallas_call(functools.partial(kernel, n, pipes, chunks, tap_count, bat...  55.4 us
    unnamed x10, local copies, waits for them, and re-layouts  5.39 us

profile of v1, /device:TPU:13, one launch (start us, length us, event | category | flops | bytes accessed | tf_op | source)
XLA Modules:
  0.0 61.4 jit_solution(11868355634945822406)
XLA Ops:
  0.6 0.0 copy-start.2
  0.6 0.7 %copy.10 = bf16[1,2,7,512]{3,2,1,0:T(8,128)(2,1)S(1)} copy(bf16[1,2,7,512]{3,1,2,0:T(2,128)(2,1)} %param.6) | data formatting | bytes 28672 | tf_op args[2]
  1.4 0.0 copy-done.2
  1.4 0.0 copy-start
  1.4 1.2 %copy-done = bf16[1,128,4096]{2,1,0:T(8,128)(2,1)S(1)} copy-done((bf16[1,128,4096]{2,1,0:T(8,128)(2,1)S(1)}, bf16[1,128,4096]{2,1,0:T(8,128)(2,1)}, u32[]{:S(2)}) %copy-start) | copy-done | bytes 1048600
  2.6 0.0 copy-start.1
  2.6 1.2 %copy-done.1 = bf16[1,128,4096]{2,1,0:T(8,128)(2,1)S(1)} copy-done((bf16[1,128,4096]{2,1,0:T(8,128)(2,1)S(1)}, bf16[1,128,4096]{2,1,0:T(8,128)(2,1)}, u32[]{:S(2)}) %copy-start.1) | copy-done | bytes 1048600
  3.8 55.4 %shard_map.67 = (bf16[128,4096]{1,0:T(8,128)(2,1)S(1)}, f32[2,7,512]{2,1,0:T(8,128)S(1)}, f32[2,32,128]{2,1,0:T(8,128)S(1)}) custom-call(bf16[128,4096]{1,0:T(8,128)(2,1)S(1)} %bitcast.11, bf16[128,4096]{1,0:T(8,128)(2,1)S(1)} %bitcast.12, bf16[2,7,512]{2,1,0:T(8,128)(2,1)S(1)} %bitcast.14, f32[2,32,128]{2,1,0:T(8,128)S(1)} %bitcast_convert_fusion.lf_ref), custom_call_target="tpu_custom_call" | custom-call | tf_op jit(solution)/shard_map/pallas_call | solution.py:286
  59.2 0.6 %copy.8 = f32[1,2,7,512]{3,1,2,0:T(2,128)} copy(f32[1,2,7,512]{3,2,1,0:T(8,128)S(1)} %bitcast.16) | data formatting | bytes 57344
  59.8 1.0 %copy.13 = bf16[1,128,4096]{2,1,0:T(8,128)(2,1)} copy(bf16[1,128,4096]{2,1,0:T(8,128)(2,1)S(1)} %bitcast.13) | data formatting | bytes 2097152
  60.8 0.6 copy.14
  (1 shorter events, 0.0 us)
Async XLA Ops:
  0.6 0.7 %copy-start.2 = (bf16[1,2,32,128]{3,2,1,0:T(8,128)(2,1)S(1)}, bf16[1,2,32,128]{3,2,1,0:T(8,128)(2,1)}, u32[]{:S(2)}) copy-start(bf16[1,2,32,128]{3,2,1,0:T(8,128)(2,1)} %param.7) | copy-start | bytes 49156
  1.4 1.2 %copy-start = (bf16[1,128,4096]{2,1,0:T(8,128)(2,1)S(1)}, bf16[1,128,4096]{2,1,0:T(8,128)(2,1)}, u32[]{:S(2)}) copy-start(bf16[1,128,4096]{2,1,0:T(8,128)(2,1)} %param.4) | copy-start | bytes 3145732
  2.6 1.2 %copy-start.1 = (bf16[1,128,4096]{2,1,0:T(8,128)(2,1)S(1)}, bf16[1,128,4096]{2,1,0:T(8,128)(2,1)}, u32[]{:S(2)}) copy-start(bf16[1,128,4096]{2,1,0:T(8,128)(2,1)} %param.5) | copy-start | bytes 3145732

commit v2 on v1

--- a/solution.py
+++ b/solution.py
@@ -47,10 +47,28 @@
     return jnp.where(lanes_of(x.shape[0]) < LANES - k, rolled, next_block(rolled))
 
 
+def flip(index, mask):
+    out = index
+    bit = 1
+    while bit <= mask:
+        if mask & bit:
+            out = out + bit - 2 * bit * lax.rem(lax.div(index, bit), 2)
+        bit *= 2
+    return out
+
+
+def orders(n):
+    far = list(range(1, n // 2))
+    later = far[1:] + far[:1]
+    even = [2 * m for m in far] + [2 * m + 1 for m in far]
+    odd = [2 * m for m in later] + [2 * m + 1 for m in later]
+    return list(zip(even + [1], odd + [1]))
+
+
 def kernel(n, pipes, chunks, tap_count, batch, factor,
            x_ref, g_ref, sf_ref, lf_ref,
            out_ref, short_ref, long_ref,
-           recv, xt, ot, obuf, zbuf, wide, now_ref, past_ref, corr, lag,
+           recv, xt, ot, obuf, zbuf, wide, now_ref, past_ref, corr, lag, lf_wide,
            send_sem, recv_sem, local_sem, osend_sem, orecv_sem, zero_sem):
     stage = lax.axis_index("pipe")
     me = lax.axis_index("dp")
@@ -73,8 +91,16 @@
     def columns(device, q):
         return pl.ds(pl.multiple_of(device * width + q * LANES, LANES), LANES)
 
-    def in_copy(a, q, j, slot):
-        to = lax.rem(me + j, n)
+    core = lax.rem(me, 2)
+
+    def pick(step):
+        first, second = step
+        return (
+            first + core * (second - first),
+            flip(me, first) + core * (flip(me, second) - flip(me, first)),
+        )
+
+    def in_copy(a, q, j, to, slot):
         return pltpu.make_async_remote_copy(
             src_ref=(x_ref, g_ref)[a].at[:, columns(to, q)],
             dst_ref=recv.at[a, q, slot],
@@ -89,8 +115,7 @@
             (x_ref, g_ref)[a].at[:, columns(me, q)], recv.at[a, q, me], local_sem.at[a, q]
         )
 
-    def out_copy(q, j, source):
-        to = lax.rem(me + j, n)
+    def out_copy(q, j, to, source):
         return pltpu.make_async_remote_copy(
             src_ref=obuf.at[q, to],
             dst_ref=out_ref.at[:, columns(source, q)],
@@ -102,9 +127,9 @@
 
     @pl.loop(0, chunks)
     def _(q):
-        for j in range(1, n):
+        for step in orders(n):
             for a in range(2):
-                in_copy(a, q, j, me).start()
+                in_copy(a, q, *pick(step), me).start()
         for a in range(2):
             own_copy(a, q).start()
 
@@ -124,15 +149,17 @@
     @pl.loop(0, chunks)
     def _(q):
         for blk in range(2):
-            taps_q = sf_ref[blk, :, pl.ds(pl.multiple_of(q * LANES, LANES), LANES)]
+            taps_q = sf_ref[:, blk, pl.ds(pl.multiple_of(q * LANES, LANES), LANES)]
             for k in range(tap_count):
                 spread = jnp.broadcast_to(taps_q[k:k + 1].astype(F32), square).astype(BF16)
                 wide[q, blk * tap_count + k] = mm(eye, spread, NT)
 
+    lf_wide[...] = lf_ref[...].astype(F32)
+
     @pl.loop(0, groups)
     def _(g):
         for blk in range(2):
-            filt = lf_ref[blk, pl.ds(g, 1)]
+            filt = lf_wide[blk, pl.ds(g, 1)]
             circ = pltpu.roll(jnp.broadcast_to(filt, square), 0, 1, stride=1, stride_axis=0)
             now_ref[blk, g] = jnp.where(upper, circ, 0.0).astype(BF16)
             past_ref[blk, g] = jnp.where(upper, 0.0, circ).astype(BF16)
@@ -184,7 +211,7 @@
     def _(q):
         for j in range(1, n):
             for a in range(2):
-                in_copy(a, q, j, lax.rem(me - j + n, n)).wait_recv()
+                in_copy(a, q, j, flip(me, j), flip(me, j)).wait_recv()
         for a in range(2):
             own_copy(a, q).wait()
         for a in range(2):
@@ -224,8 +251,8 @@
             for b in range(n):
                 piece = ot[:, b * PER_GROUP:(b + 1) * PER_GROUP, :].reshape(square)
                 obuf[q, b] = mm(eye, piece, NT).astype(BF16)
-            for j in range(n):
-                out_copy(q, j, me).start()
+            for step in orders(n) + [(0, 0)]:
+                out_copy(q, *pick(step), me).start()
 
         ones = jnp.ones((8, 2 * LANES), BF16)
         for blk in range(2):
@@ -234,7 +261,7 @@
                 high = part.astype(BF16)
                 low = (part - high.astype(F32)).astype(BF16)
                 summed = mm(ones, jnp.concatenate([high, low], axis=1), NT)
-                short_ref[blk, k:k + 1, pl.ds(pl.multiple_of(q * LANES, LANES), LANES)] = (
+                short_ref[k, blk:blk + 1, pl.ds(pl.multiple_of(q * LANES, LANES), LANES)] = (
                     summed[:1] * factor
                 )
 
@@ -249,7 +276,7 @@
     def _(q):
         for j in range(1, n):
             for a in range(2):
-                in_copy(a, q, j, me).wait_send()
+                in_copy(a, q, j, flip(me, j), me).wait_send()
 
     @pl.when(stage == pipes - 1)
     def _():
@@ -260,14 +287,14 @@
         @pl.loop(0, chunks)
         def _(q):
             for j in range(n):
-                out_copy(q, j, me).wait_send()
+                out_copy(q, j, flip(me, j), me).wait_send()
 
     @pl.when(stage < pipes - 1)
     def _():
         @pl.loop(0, chunks)
         def _(q):
             for j in range(n):
-                out_copy(q, j, lax.rem(me - j + n, n)).wait_recv()
+                out_copy(q, j, flip(me, j), flip(me, j)).wait_recv()
 
 
 def body(n, pipes, section_input, out_grad, short_filter, long_filter):
@@ -281,13 +308,13 @@
     batch = max(1, min(4, 32 // n))
     factor = float(rows * n) ** (-0.5)
     vmem = pl.BlockSpec(memory_space=pltpu.VMEM)
-    anywhere = pl.BlockSpec(memory_space=pl.ANY)
+    anywhere = pl.BlockSpec(memory_space=pltpu.HBM)
     dma = pltpu.SemaphoreType.DMA
     passed, short_grad, long_grad = pl.pallas_call(
         functools.partial(kernel, n, pipes, chunks, tap_count, batch, factor),
         out_shape=(
             jax.ShapeDtypeStruct((rows, channels), BF16),
-            jax.ShapeDtypeStruct((2, tap_count, width), F32),
+            jax.ShapeDtypeStruct((tap_count, 2, width), F32),
             jax.ShapeDtypeStruct((2, groups, taps), F32),
         ),
         in_specs=[anywhere, anywhere, vmem, vmem],
@@ -303,6 +330,7 @@
             pltpu.VMEM((2, groups, LANES, LANES), BF16),
             pltpu.VMEM((2 * tap_count, LANES, LANES), F32),
             pltpu.VMEM((2 * groups * 8, LANES), F32),
+            pltpu.VMEM((2, groups, LANES), F32),
             dma((2, chunks, n)),
             dma((2, chunks, n)),
             dma((2, chunks)),
@@ -311,10 +339,10 @@
             dma(()),
         ],
         compiler_params=pltpu.CompilerParams(
-            collective_id=0, has_side_effects=True, vmem_limit_bytes=48 * 1024 * 1024
+            collective_id=0, has_side_effects=True, vmem_limit_bytes=63 * 1024 * 1024
         ),
-    )(section_input[0], out_grad[0], short_filter[0], long_filter[0].astype(F32))
-    return passed[None], short_grad[None], long_grad[None]
+    )(section_input[0], out_grad[0], short_filter[0].transpose(1, 0, 2), long_filter[0])
+    return passed[None], short_grad.transpose(1, 0, 2)[None], long_grad[None]
 
 
 def solution(mesh):

time: 61.7 us -> 57.7 us (0.935)
  Pallas kernels: 55.4 us -> 52.8 us
  local copies, waits for them, and re-layouts: 5.39 us -> 3.68 us
    pallas_call x1, Pallas kernels: 55.4 us -> 52.8 us  [body(): pl.pallas_call(functools.partial(kernel, n, pipes, chunks, tap_count, bat...]
    unnamed x10 -> x7, local copies, waits for them, and re-layouts: 5.39 us -> 3.68 us
where the time goes in v2:
time: 57.7 us; the launch traced here: 57.2 us
  Pallas kernels  52.8 us (92%)
  local copies, waits for them, and re-layouts  3.68 us (6%)
  between operations  0.65 us (1%)
    pallas_call x1, Pallas kernels, body(): pl.pallas_call(functools.partial(kernel, n, pipes, chunks, tap_count, bat...  52.8 us
    unnamed x7, local copies, waits for them, and re-layouts  3.68 us

profile of v2, /device:TPU:13, one launch (start us, length us, event | category | flops | bytes accessed | tf_op | source)
XLA Modules:
  0.0 57.2 jit_solution(4706259308526256917)
XLA Ops:
  0.6 52.8 %shard_map.67 = (bf16[128,4096]{1,0:T(8,128)(2,1)}, f32[7,2,512]{2,1,0:T(2,128)}, f32[2,32,128]{2,1,0:T(8,128)}) custom-call(bf16[128,4096]{1,0:T(8,128)(2,1)} %bitcast.11, bf16[128,4096]{1,0:T(8,128)(2,1)} %bitcast.12, bf16[7,2,512]{2,1,0:T(2,128)(2,1)} %bitcast.17, bf16[2,32,128]{2,1,0:T(8,128)(2,1)} %bitcast.16), custom_call_target="tpu_custom_call" | custom-call | tf_op jit(solution)/shard_map/pallas_call | solution.py:313
  53.5 0.0 copy-start.1
  53.5 2.3 %copy.10 = bf16[1,128,4096]{2,1,0:T(8,128)(2,1)} copy(bf16[1,128,4096]{2,1,0:T(8,128)(2,1)} %bitcast.13) | data formatting | bytes 2097152
  55.8 0.0 copy-done.1
  55.8 0.0 copy-start
  55.8 0.6 %copy.11 = f32[1,2,7,512]{3,1,2,0:T(2,128)} copy(f32[1,2,7,512]{3,1,2,0:T(2,128)S(1)} %bitcast.15) | data formatting | bytes 57344
  56.4 0.2 copy-done
  56.6 0.6 %copy.12 = f32[1,2,32,128]{3,2,1,0:T(8,128)} copy(f32[1,2,32,128]{3,2,1,0:T(8,128)S(1)} %bitcast.14) | data formatting | bytes 65536
Async XLA Ops:
  53.5 2.3 %copy-start.1 = (f32[7,2,512]{2,1,0:T(2,128)S(1)}, f32[7,2,512]{2,1,0:T(2,128)}, u32[]{:S(2)}) copy-start(f32[7,2,512]{2,1,0:T(2,128)} %get-tuple-element.7) | copy-start | bytes 86020
  55.8 0.8 %copy-start = (f32[2,32,128]{2,1,0:T(8,128)S(1)}, f32[2,32,128]{2,1,0:T(8,128)}, u32[]{:S(2)}) copy-start(f32[2,32,128]{2,1,0:T(8,128)} %get-tuple-element.8) | copy-start | bytes 98308

commit v3 on v2

--- a/solution.py
+++ b/solution.py
@@ -68,8 +68,8 @@
 def kernel(n, pipes, chunks, tap_count, batch, factor,
            x_ref, g_ref, sf_ref, lf_ref,
            out_ref, short_ref, long_ref,
-           recv, xt, ot, obuf, zbuf, wide, now_ref, past_ref, corr, lag, lf_wide,
-           send_sem, recv_sem, local_sem, osend_sem, orecv_sem, zero_sem):
+           recv, xt, ot, obuf, wide, now_ref, past_ref, corr, lag, lf_wide, mix_ref, back_ref,
+           send_sem, recv_sem, local_sem, osend_sem, orecv_sem):
     stage = lax.axis_index("pipe")
     me = lax.axis_index("dp")
     rows = x_ref.shape[0]
@@ -133,13 +133,6 @@
         for a in range(2):
             own_copy(a, q).start()
 
-    zero_copy = pltpu.make_async_copy(zbuf, out_ref, zero_sem)
-
-    @pl.when(stage == pipes - 1)
-    def _():
-        zbuf[...] = jnp.zeros_like(zbuf)
-        zero_copy.start()
-
     square = (LANES, LANES)
     row_pos = lax.broadcasted_iota(jnp.int32, square, 0)
     col_pos = lax.broadcasted_iota(jnp.int32, square, 1)
@@ -152,7 +145,18 @@
             taps_q = sf_ref[:, blk, pl.ds(pl.multiple_of(q * LANES, LANES), LANES)]
             for k in range(tap_count):
                 spread = jnp.broadcast_to(taps_q[k:k + 1].astype(F32), square).astype(BF16)
-                wide[q, blk * tap_count + k] = mm(eye, spread, NT)
+                wide[q, blk * tap_count + k] = mm(eye, spread, NT).astype(BF16)
+
+    wide_row = lax.broadcasted_iota(jnp.int32, (LANES, 2 * LANES), 0)
+    wide_col = lax.broadcasted_iota(jnp.int32, (LANES, 2 * LANES), 1)
+    for k in range(tap_count):
+        at = pl.ds(k * LANES, LANES)
+        mix_ref[at] = (wide_col == wide_row + k).astype(BF16)
+        away = jnp.where(wide_col < LANES, wide_col + k, wide_col - 2 * LANES + k)
+        back_ref[at] = (wide_row == away).astype(BF16)
+    fold_row = lax.broadcasted_iota(jnp.int32, (PER_GROUP, n * PER_GROUP), 0)
+    fold_col = lax.broadcasted_iota(jnp.int32, (PER_GROUP, n * PER_GROUP), 1)
+    fold = (lax.rem(fold_col, PER_GROUP) == fold_row).astype(BF16)
 
     lf_wide[...] = lf_ref[...].astype(F32)
 
@@ -188,24 +192,35 @@
         one = wide[q, blk * tap_count + k, pl.ds(pl.multiple_of(gl * PER_GROUP, PER_GROUP), PER_GROUP)]
         return jnp.concatenate([one] * n, axis=0)
 
-    def short_mix(x, q, gl, blk):
-        total = tap(q, gl, blk, 0) * x
-        for k in range(1, tap_count):
-            total = total + tap(q, gl, blk, k) * shift_past(x, k)
-        return total.astype(BF16)
-
-    def short_back(base, d, x, q, gl, blk):
-        total = base
+    def weighted(x, q, gl, blk):
+        return jnp.concatenate([tap(q, gl, blk, k) * x for k in range(tap_count)], axis=1)
+
+    def short_mix(xs, q, local, blk):
+        terms = jnp.concatenate([weighted(x, q, gl, blk) for x, gl in zip(xs, local)], axis=0)
+        both = mm(terms, mix_ref[...], NN)
+        size = n * PER_GROUP
+        return [
+            (both[u * size:(u + 1) * size, :LANES]
+             + past_block(both[u * size:(u + 1) * size, LANES:])).astype(BF16)
+            for u in range(len(xs))
+        ]
+
+    def short_back(bases, ds, q, local, blk):
+        terms = jnp.concatenate([weighted(d, q, gl, blk) for d, gl in zip(ds, local)], axis=0)
+        both = mm(terms, back_ref[...], NN)
+        size = n * PER_GROUP
+        return [
+            (base.astype(F32) + both[u * size:(u + 1) * size, :LANES]
+             + next_block(both[u * size:(u + 1) * size, LANES:])).astype(BF16)
+            for u, base in enumerate(bases)
+        ]
+
+    def short_corr(d, x, gl, blk):
         at = pl.ds(pl.multiple_of(gl * PER_GROUP, PER_GROUP), PER_GROUP)
+        prods = jnp.concatenate([shift_next(d, k) * x for k in range(tap_count)], axis=1)
+        sums = mm(fold, prods, NN)
         for k in range(tap_count):
-            moved = shift_next(d, k)
-            total = total + tap(q, gl, blk, k) * moved
-            prod = moved * x
-            part = prod[:PER_GROUP]
-            for b in range(1, n):
-                part = part + prod[b * PER_GROUP:(b + 1) * PER_GROUP]
-            corr[blk * tap_count + k, at] = part
-        return total.astype(BF16)
+            corr[blk * tap_count + k, at] = sums[:, k * LANES:(k + 1) * LANES]
 
     @pl.loop(0, chunks)
     def _(q):
@@ -227,22 +242,23 @@
             every = range(batch)
             glob = [q * per_chunk + gl for gl in local]
             top = [xt[1, gl] for gl in local]
-            src = [xt[0, gl].astype(F32) for gl in local]
-            dmix_two = [anti(top[u], 1, glob[u]).astype(BF16).astype(F32) for u in every]
-            mixed_one = [short_mix(src[u], q, local[u], 0) for u in every]
+            src = [xt[0, gl] for gl in local]
+            dmix_two = [anti(top[u], 1, glob[u]).astype(BF16) for u in every]
+            mixed_one = short_mix(src, q, local, 0)
             long_one = [causal(mixed_one[u], 0, glob[u]) for u in every]
-            middle = [(src[u] + long_one[u]).astype(BF16).astype(F32) for u in every]
-            middle_grad = [
-                short_back(top[u].astype(F32), dmix_two[u], middle[u], q, local[u], 1) for u in every
-            ]
-            dmix_one = [anti(middle_grad[u], 0, glob[u]).astype(BF16).astype(F32) for u in every]
-            mixed_two = [short_mix(middle[u], q, local[u], 1) for u in every]
+            middle = [(src[u].astype(F32) + long_one[u]).astype(BF16) for u in every]
+            middle_grad = short_back(top, dmix_two, q, local, 1)
+            dmix_one = [anti(middle_grad[u], 0, glob[u]).astype(BF16) for u in every]
+            mixed_two = short_mix(middle, q, local, 1)
+            for u in every:
+                short_corr(dmix_two[u], middle[u], local[u], 1)
             for u in every:
                 lag_part(mixed_two[u], top[u], 1, glob[u])
-            for u in every:
-                ot[local[u]] = short_back(
-                    middle_grad[u].astype(F32), dmix_one[u], src[u], q, local[u], 0
-                )
+            result = short_back(middle_grad, dmix_one, q, local, 0)
+            for u in every:
+                ot[local[u]] = result[u]
+            for u in every:
+                short_corr(dmix_one[u], src[u], local[u], 0)
             for u in every:
                 lag_part(mixed_one[u], middle_grad[u], 0, glob[u])
 
@@ -277,10 +293,6 @@
         for j in range(1, n):
             for a in range(2):
                 in_copy(a, q, j, flip(me, j), me).wait_send()
-
-    @pl.when(stage == pipes - 1)
-    def _():
-        zero_copy.wait()
 
     @pl.when(stage > 0)
     def _():
@@ -324,24 +336,25 @@
             pltpu.VMEM((2, per_chunk, n * PER_GROUP, LANES), BF16),
             pltpu.VMEM((per_chunk, n * PER_GROUP, LANES), BF16),
             pltpu.VMEM((chunks, n, LANES, LANES), BF16),
-            pltpu.VMEM((rows, channels), BF16),
-            pltpu.VMEM((chunks, 2 * tap_count, LANES, LANES), F32),
+            pltpu.VMEM((chunks, 2 * tap_count, LANES, LANES), BF16),
             pltpu.VMEM((2, groups, LANES, LANES), BF16),
             pltpu.VMEM((2, groups, LANES, LANES), BF16),
             pltpu.VMEM((2 * tap_count, LANES, LANES), F32),
             pltpu.VMEM((2 * groups * 8, LANES), F32),
             pltpu.VMEM((2, groups, LANES), F32),
+            pltpu.VMEM((tap_count * LANES, 2 * LANES), BF16),
+            pltpu.VMEM((tap_count * LANES, 2 * LANES), BF16),
             dma((2, chunks, n)),
             dma((2, chunks, n)),
             dma((2, chunks)),
             dma((chunks, n)),
             dma((chunks, n)),
-            dma(()),
         ],
         compiler_params=pltpu.CompilerParams(
             collective_id=0, has_side_effects=True, vmem_limit_bytes=63 * 1024 * 1024
         ),
     )(section_input[0], out_grad[0], short_filter[0].transpose(1, 0, 2), long_filter[0])
+    passed = jnp.where(lax.axis_index("pipe") < pipes - 1, passed, jnp.zeros_like(passed))
     return passed[None], short_grad.transpose(1, 0, 2)[None], long_grad[None]
 
 

time: 57.7 us -> 56.4 us (0.977)
  the two profiles are of different devices: /device:TPU:13 before, /device:TPU:0 now
where the time goes in v3:
time: 56.4 us; the launch traced here: 56.1 us
  Pallas kernels  51.7 us (92%)
  other arithmetic  2.28 us (4%)
  local copies, waits for them, and re-layouts  1.38 us (2%)
  between operations  0.66 us (1%)
    pallas_call x1, Pallas kernels, body(): pl.pallas_call(functools.partial(kernel, n, pipes, chunks, tap_count, bat...  51.7 us
    broadcast_in_dim x1, other arithmetic, body(): return (passed[None], short_grad.transpose(1, 0, 2)[None], long_grad[None])  2.28 us
    unnamed x6, local copies, waits for them, and re-layouts  1.38 us

profile of v3, /device:TPU:0, one launch (start us, length us, event | category | flops | bytes accessed | tf_op | source)
XLA Modules:
  0.0 56.1 jit_solution(786116482051299852)
XLA Ops:
  0.6 51.7 %shard_map.67 = (bf16[128,4096]{1,0:T(8,128)(2,1)}, f32[7,2,512]{2,1,0:T(2,128)}, f32[2,32,128]{2,1,0:T(8,128)}) custom-call(bf16[128,4096]{1,0:T(8,128)(2,1)} %bitcast.12, bf16[128,4096]{1,0:T(8,128)(2,1)} %bitcast.13, bf16[7,2,512]{2,1,0:T(2,128)(2,1)} %bitcast.17, bf16[2,32,128]{2,1,0:T(8,128)(2,1)} %bitcast.16), custom_call_target="tpu_custom_call" | custom-call | tf_op jit(solution)/shard_map/pallas_call | solution.py:325
  52.4 0.0 copy-start.1
  52.4 2.3 %select_bitcast_fusion = bf16[1,128,4096]{2,1,0:T(8,128)(2,1)} fusion(bf16[128,4096]{1,0:T(8,128)(2,1)} %get-tuple-element.6, pred[]{:T(512)S(6)} %lt.3), kind=kLoop, calls=%fused_computation | loop fusion | flops 524288 | bytes 2097153 | tf_op jit(solution)/shard_map/broadcast_in_dim | solution.py:358
  54.7 0.0 copy-start
  54.7 0.0 copy-done.1
  54.7 0.6 %copy.9 = f32[1,2,7,512]{3,1,2,0:T(2,128)} copy(f32[1,2,7,512]{3,1,2,0:T(2,128)S(1)} %bitcast.15) | data formatting | bytes 57344
  55.3 0.2 copy-done
  55.5 0.6 %copy.10 = f32[1,2,32,128]{3,2,1,0:T(8,128)} copy(f32[1,2,32,128]{3,2,1,0:T(8,128)S(1)} %bitcast.14) | data formatting | bytes 65536
Async XLA Ops:
  52.4 2.3 %copy-start.1 = (f32[7,2,512]{2,1,0:T(2,128)S(1)}, f32[7,2,512]{2,1,0:T(2,128)}, u32[]{:S(2)}) copy-start(f32[7,2,512]{2,1,0:T(2,128)} %get-tuple-element.7) | copy-start | bytes 86020
  54.7 0.8 %copy-start = (f32[2,32,128]{2,1,0:T(8,128)S(1)}, f32[2,32,128]{2,1,0:T(8,128)}, u32[]{:S(2)}) copy-start(f32[2,32,128]{2,1,0:T(8,128)} %get-tuple-element.8) | copy-start | bytes 98308

commit v4 on v3

--- a/solution.py
+++ b/solution.py
@@ -68,7 +68,7 @@
 def kernel(n, pipes, chunks, tap_count, batch, factor,
            x_ref, g_ref, sf_ref, lf_ref,
            out_ref, short_ref, long_ref,
-           recv, xt, ot, obuf, wide, now_ref, past_ref, corr, lag, lf_wide, mix_ref, back_ref,
+           recv, xt, ot, obuf, wide, now_ref, past_ref, corr, lag, lf_wide, mix_ref,
            send_sem, recv_sem, local_sem, osend_sem, orecv_sem):
     stage = lax.axis_index("pipe")
     me = lax.axis_index("dp")
@@ -152,8 +152,6 @@
     for k in range(tap_count):
         at = pl.ds(k * LANES, LANES)
         mix_ref[at] = (wide_col == wide_row + k).astype(BF16)
-        away = jnp.where(wide_col < LANES, wide_col + k, wide_col - 2 * LANES + k)
-        back_ref[at] = (wide_row == away).astype(BF16)
     fold_row = lax.broadcasted_iota(jnp.int32, (PER_GROUP, n * PER_GROUP), 0)
     fold_col = lax.broadcasted_iota(jnp.int32, (PER_GROUP, n * PER_GROUP), 1)
     fold = (lax.rem(fold_col, PER_GROUP) == fold_row).astype(BF16)
@@ -205,22 +203,16 @@
             for u in range(len(xs))
         ]
 
-    def short_back(bases, ds, q, local, blk):
-        terms = jnp.concatenate([weighted(d, q, gl, blk) for d, gl in zip(ds, local)], axis=0)
-        both = mm(terms, back_ref[...], NN)
-        size = n * PER_GROUP
-        return [
-            (base.astype(F32) + both[u * size:(u + 1) * size, :LANES]
-             + next_block(both[u * size:(u + 1) * size, LANES:])).astype(BF16)
-            for u, base in enumerate(bases)
-        ]
-
-    def short_corr(d, x, gl, blk):
+    def short_back(base, d, x, q, gl, blk):
         at = pl.ds(pl.multiple_of(gl * PER_GROUP, PER_GROUP), PER_GROUP)
-        prods = jnp.concatenate([shift_next(d, k) * x for k in range(tap_count)], axis=1)
-        sums = mm(fold, prods, NN)
+        moved = [shift_next(d, k) for k in range(tap_count)]
+        total = base.astype(F32)
+        for k in range(tap_count):
+            total = total + tap(q, gl, blk, k).astype(F32) * moved[k].astype(F32)
+        sums = mm(fold, jnp.concatenate([m * x for m in moved], axis=1), NN)
         for k in range(tap_count):
             corr[blk * tap_count + k, at] = sums[:, k * LANES:(k + 1) * LANES]
+        return total.astype(BF16)
 
     @pl.loop(0, chunks)
     def _(q):
@@ -247,18 +239,15 @@
             mixed_one = short_mix(src, q, local, 0)
             long_one = [causal(mixed_one[u], 0, glob[u]) for u in every]
             middle = [(src[u].astype(F32) + long_one[u]).astype(BF16) for u in every]
-            middle_grad = short_back(top, dmix_two, q, local, 1)
+            middle_grad = [
+                short_back(top[u], dmix_two[u], middle[u], q, local[u], 1) for u in every
+            ]
             dmix_one = [anti(middle_grad[u], 0, glob[u]).astype(BF16) for u in every]
             mixed_two = short_mix(middle, q, local, 1)
             for u in every:
-                short_corr(dmix_two[u], middle[u], local[u], 1)
+                lag_part(mixed_two[u], top[u], 1, glob[u])
             for u in every:
-                lag_part(mixed_two[u], top[u], 1, glob[u])
-            result = short_back(middle_grad, dmix_one, q, local, 0)
-            for u in every:
-                ot[local[u]] = result[u]
-            for u in every:
-                short_corr(dmix_one[u], src[u], local[u], 0)
+                ot[local[u]] = short_back(middle_grad[u], dmix_one[u], src[u], q, local[u], 0)
             for u in every:
                 lag_part(mixed_one[u], middle_grad[u], 0, glob[u])
 
@@ -309,6 +298,42 @@
                 out_copy(q, j, flip(me, j), flip(me, j)).wait_recv()
 
 
+def finish(pipes, passed_ref, short_ref, long_ref, out_ref, short_out, long_out, zeros, sem, sem_s, sem_l):
+    stage = lax.axis_index("pipe")
+    parts = sem.shape[0]
+    size = passed_ref.shape[0] // parts
+    small = [
+        pltpu.make_async_copy(short_ref, short_out, sem_s),
+        pltpu.make_async_copy(long_ref, long_out, sem_l),
+    ]
+    for copy in small:
+        copy.start()
+
+    def move(source):
+        copies = [
+            pltpu.make_async_copy(
+                source.at[pl.ds(i * size, size)], out_ref.at[pl.ds(i * size, size)], sem.at[i]
+            )
+            for i in range(parts)
+        ]
+        for copy in copies:
+            copy.start()
+        for copy in copies:
+            copy.wait()
+
+    @pl.when(stage < pipes - 1)
+    def _():
+        move(passed_ref)
+
+    @pl.when(stage == pipes - 1)
+    def _():
+        zeros[...] = jnp.zeros_like(zeros)
+        move(zeros)
+
+    for copy in small:
+        copy.wait()
+
+
 def body(n, pipes, section_input, out_grad, short_filter, long_filter):
     rows, channels = section_input.shape[1:]
     tap_count = short_filter.shape[2]
@@ -317,7 +342,7 @@
     chunks = width // LANES
     assert rows == LANES and taps == LANES and width == groups * PER_GROUP
     per_chunk = LANES // PER_GROUP
-    batch = max(1, min(4, 32 // n))
+    batch = max(1, min(8, 64 // n))
     factor = float(rows * n) ** (-0.5)
     vmem = pl.BlockSpec(memory_space=pltpu.VMEM)
     anywhere = pl.BlockSpec(memory_space=pltpu.HBM)
@@ -343,7 +368,6 @@
             pltpu.VMEM((2 * groups * 8, LANES), F32),
             pltpu.VMEM((2, groups, LANES), F32),
             pltpu.VMEM((tap_count * LANES, 2 * LANES), BF16),
-            pltpu.VMEM((tap_count * LANES, 2 * LANES), BF16),
             dma((2, chunks, n)),
             dma((2, chunks, n)),
             dma((2, chunks)),
@@ -354,7 +378,14 @@
             collective_id=0, has_side_effects=True, vmem_limit_bytes=63 * 1024 * 1024
         ),
     )(section_input[0], out_grad[0], short_filter[0].transpose(1, 0, 2), long_filter[0])
-    passed = jnp.where(lax.axis_index("pipe") < pipes - 1, passed, jnp.zeros_like(passed))
+    passed, short_grad, long_grad = pl.pallas_call(
+        functools.partial(finish, pipes),
+        out_shape=tuple(jax.ShapeDtypeStruct(x.shape, x.dtype) for x in (passed, short_grad, long_grad)),
+        in_specs=[anywhere] * 3,
+        out_specs=(anywhere,) * 3,
+        scratch_shapes=[pltpu.VMEM((rows, channels), BF16), dma((8,)), dma(()), dma(())],
+        compiler_params=pltpu.CompilerParams(vmem_limit_bytes=63 * 1024 * 1024),
+    )(passed, short_grad, long_grad)
     return passed[None], short_grad.transpose(1, 0, 2)[None], long_grad[None]
 
 

time: 56.4 us -> 88.7 us (1.57)
  the two profiles are of different devices: /device:TPU:0 before, /device:TPU:13 now
where the time goes in v4:
time: 88.7 us; the launch traced here: 88.2 us
  Pallas kernels  87.6 us (99%)
    pallas_call x1, Pallas kernels, body(): pl.pallas_call(functools.partial(kernel, n, pipes, chunks, tap_count, bat...  52.8 us
    pallas_call x1, Pallas kernels, body(): pl.pallas_call(functools.partial(finish, pipes), out_shape=tuple((jax.Sha...  34.8 us

profile of v4, /device:TPU:13, one launch (start us, length us, event | category | flops | bytes accessed | tf_op | source)
XLA Modules:
  0.0 88.2 jit_solution(9328314732381829054)
XLA Ops:
  0.6 52.8 %shard_map.67 = (bf16[128,4096]{1,0:T(8,128)(2,1)}, f32[7,2,512]{2,1,0:T(2,128)}, f32[2,32,128]{2,1,0:T(8,128)}) custom-call(bf16[128,4096]{1,0:T(8,128)(2,1)} %bitcast.11, bf16[128,4096]{1,0:T(8,128)(2,1)} %bitcast.12, bf16[7,2,512]{2,1,0:T(2,128)(2,1)} %bitcast.14, bf16[2,32,128]{2,1,0:T(8,128)(2,1)} %bitcast.13), custom_call_target="tpu_custom_call" | custom-call | tf_op jit(solution)/shard_map/pallas_call | solution.py:350
  53.4 34.8 %shard_map.68 = (bf16[128,4096]{1,0:T(8,128)(2,1)}, f32[7,2,512]{2,1,0:T(2,128)}, f32[2,32,128]{2,1,0:T(8,128)}) custom-call(bf16[128,4096]{1,0:T(8,128)(2,1)} %get-tuple-element.9.passed_ref, f32[7,2,512]{2,1,0:T(2,128)} %get-tuple-element.10.short_ref, f32[2,32,128]{2,1,0:T(8,128)} %get-tuple-element.11.long_ref), custom_call_target="tpu_custom_call" | custom-call | tf_op jit(solution)/shard_map/pallas_call | solution.py:381

commit v5 on v4

--- a/solution.py
+++ b/solution.py
@@ -68,8 +68,8 @@
 def kernel(n, pipes, chunks, tap_count, batch, factor,
            x_ref, g_ref, sf_ref, lf_ref,
            out_ref, short_ref, long_ref,
-           recv, xt, ot, obuf, wide, now_ref, past_ref, corr, lag, lf_wide, mix_ref,
-           send_sem, recv_sem, local_sem, osend_sem, orecv_sem):
+           recv, sbuf, xt, ot, obuf, wide, now_ref, past_ref, corr, lag, lf_wide,
+           send_sem, recv_sem, stage_sem, local_sem, osend_sem, orecv_sem):
     stage = lax.axis_index("pipe")
     me = lax.axis_index("dp")
     rows = x_ref.shape[0]
@@ -77,17 +77,6 @@
     per_chunk = LANES // PER_GROUP
     groups = chunks * per_chunk
 
-    barrier = pltpu.get_barrier_semaphore()
-    for j in range(1, n):
-        pl.semaphore_signal(barrier, inc=1, device_id=(stage, lax.rem(me + j, n)), device_id_type=MESH)
-
-    @pl.when(stage < pipes - 1)
-    def _():
-        for j in range(n):
-            pl.semaphore_signal(barrier, inc=1, device_id=(stage + 1, j), device_id_type=MESH)
-
-    pl.semaphore_wait(barrier, n - 1 + n * jnp.minimum(stage, 1))
-
     def columns(device, q):
         return pl.ds(pl.multiple_of(device * width + q * LANES, LANES), LANES)
 
@@ -102,7 +91,7 @@
 
     def in_copy(a, q, j, to, slot):
         return pltpu.make_async_remote_copy(
-            src_ref=(x_ref, g_ref)[a].at[:, columns(to, q)],
+            src_ref=sbuf.at[a, q, j],
             dst_ref=recv.at[a, q, slot],
             send_sem=send_sem.at[a, q, j],
             recv_sem=recv_sem.at[a, q, j],
@@ -110,6 +99,11 @@
             device_id_type=MESH,
         )
 
+    def stage_copy(a, q, j, to):
+        return pltpu.make_async_copy(
+            (x_ref, g_ref)[a].at[:, columns(to, q)], sbuf.at[a, q, j], stage_sem.at[a, q, j]
+        )
+
     def own_copy(a, q):
         return pltpu.make_async_copy(
             (x_ref, g_ref)[a].at[:, columns(me, q)], recv.at[a, q, me], local_sem.at[a, q]
@@ -118,7 +112,7 @@
     def out_copy(q, j, to, source):
         return pltpu.make_async_remote_copy(
             src_ref=obuf.at[q, to],
-            dst_ref=out_ref.at[:, columns(source, q)],
+            dst_ref=out_ref.at[source, q],
             send_sem=osend_sem.at[q, j],
             recv_sem=orecv_sem.at[q, j],
             device_id=(stage - 1, to),
@@ -129,9 +123,27 @@
     def _(q):
         for step in orders(n):
             for a in range(2):
-                in_copy(a, q, *pick(step), me).start()
+                stage_copy(a, q, *pick(step)).start()
         for a in range(2):
             own_copy(a, q).start()
+
+    barrier = pltpu.get_barrier_semaphore()
+    for j in range(1, n):
+        pl.semaphore_signal(barrier, inc=1, device_id=(stage, lax.rem(me + j, n)), device_id_type=MESH)
+
+    @pl.when(stage < pipes - 1)
+    def _():
+        for j in range(n):
+            pl.semaphore_signal(barrier, inc=1, device_id=(stage + 1, j), device_id_type=MESH)
+
+    pl.semaphore_wait(barrier, n - 1 + n * jnp.minimum(stage, 1))
+
+    @pl.loop(0, chunks)
+    def _(q):
+        for step in orders(n):
+            for a in range(2):
+                stage_copy(a, q, *pick(step)).wait()
+                in_copy(a, q, *pick(step), me).start()
 
     square = (LANES, LANES)
     row_pos = lax.broadcasted_iota(jnp.int32, square, 0)
@@ -147,11 +159,6 @@
                 spread = jnp.broadcast_to(taps_q[k:k + 1].astype(F32), square).astype(BF16)
                 wide[q, blk * tap_count + k] = mm(eye, spread, NT).astype(BF16)
 
-    wide_row = lax.broadcasted_iota(jnp.int32, (LANES, 2 * LANES), 0)
-    wide_col = lax.broadcasted_iota(jnp.int32, (LANES, 2 * LANES), 1)
-    for k in range(tap_count):
-        at = pl.ds(k * LANES, LANES)
-        mix_ref[at] = (wide_col == wide_row + k).astype(BF16)
     fold_row = lax.broadcasted_iota(jnp.int32, (PER_GROUP, n * PER_GROUP), 0)
     fold_col = lax.broadcasted_iota(jnp.int32, (PER_GROUP, n * PER_GROUP), 1)
     fold = (lax.rem(fold_col, PER_GROUP) == fold_row).astype(BF16)
@@ -190,18 +197,11 @@
         one = wide[q, blk * tap_count + k, pl.ds(pl.multiple_of(gl * PER_GROUP, PER_GROUP), PER_GROUP)]
         return jnp.concatenate([one] * n, axis=0)
 
-    def weighted(x, q, gl, blk):
-        return jnp.concatenate([tap(q, gl, blk, k) * x for k in range(tap_count)], axis=1)
-
-    def short_mix(xs, q, local, blk):
-        terms = jnp.concatenate([weighted(x, q, gl, blk) for x, gl in zip(xs, local)], axis=0)
-        both = mm(terms, mix_ref[...], NN)
-        size = n * PER_GROUP
-        return [
-            (both[u * size:(u + 1) * size, :LANES]
-             + past_block(both[u * size:(u + 1) * size, LANES:])).astype(BF16)
-            for u in range(len(xs))
-        ]
+    def short_mix(x, q, gl, blk):
+        total = tap(q, gl, blk, 0).astype(F32) * x.astype(F32)
+        for k in range(1, tap_count):
+            total = total + tap(q, gl, blk, k).astype(F32) * shift_past(x, k).astype(F32)
+        return total.astype(BF16)
 
     def short_back(base, d, x, q, gl, blk):
         at = pl.ds(pl.multiple_of(gl * PER_GROUP, PER_GROUP), PER_GROUP)
@@ -236,14 +236,14 @@
             top = [xt[1, gl] for gl in local]
             src = [xt[0, gl] for gl in local]
             dmix_two = [anti(top[u], 1, glob[u]).astype(BF16) for u in every]
-            mixed_one = short_mix(src, q, local, 0)
+            mixed_one = [short_mix(src[u], q, local[u], 0) for u in every]
             long_one = [causal(mixed_one[u], 0, glob[u]) for u in every]
             middle = [(src[u].astype(F32) + long_one[u]).astype(BF16) for u in every]
             middle_grad = [
                 short_back(top[u], dmix_two[u], middle[u], q, local[u], 1) for u in every
             ]
             dmix_one = [anti(middle_grad[u], 0, glob[u]).astype(BF16) for u in every]
-            mixed_two = short_mix(middle, q, local, 1)
+            mixed_two = [short_mix(middle[u], q, local[u], 1) for u in every]
             for u in every:
                 lag_part(mixed_two[u], top[u], 1, glob[u])
             for u in every:
@@ -298,40 +298,46 @@
                 out_copy(q, j, flip(me, j), flip(me, j)).wait_recv()
 
 
-def finish(pipes, passed_ref, short_ref, long_ref, out_ref, short_out, long_out, zeros, sem, sem_s, sem_l):
+def finish(pipes, parts_ref, short_ref, long_ref, out_ref, short_out, long_out, rows_ref, in_sem, out_sem):
     stage = lax.axis_index("pipe")
-    parts = sem.shape[0]
-    size = passed_ref.shape[0] // parts
-    small = [
-        pltpu.make_async_copy(short_ref, short_out, sem_s),
-        pltpu.make_async_copy(long_ref, long_out, sem_l),
-    ]
-    for copy in small:
-        copy.start()
-
-    def move(source):
-        copies = [
-            pltpu.make_async_copy(
-                source.at[pl.ds(i * size, size)], out_ref.at[pl.ds(i * size, size)], sem.at[i]
-            )
-            for i in range(parts)
-        ]
-        for copy in copies:
-            copy.start()
-        for copy in copies:
-            copy.wait()
+    n, chunks = parts_ref.shape[:2]
+    width = chunks * LANES
+
+    def columns(source):
+        return pl.ds(source * width, width)
+
+    def load(source, q):
+        return pltpu.make_async_copy(
+            parts_ref.at[source, q],
+            rows_ref.at[:, pl.ds(source * width + q * LANES, LANES)],
+            in_sem.at[source, q],
+        )
+
+    def store(source):
+        return pltpu.make_async_copy(
+            rows_ref.at[:, columns(source)], out_ref.at[:, columns(source)], out_sem.at[source]
+        )
 
     @pl.when(stage < pipes - 1)
     def _():
-        move(passed_ref)
+        for source in range(n):
+            for q in range(chunks):
+                load(source, q).start()
+        for source in range(n):
+            for q in range(chunks):
+                load(source, q).wait()
+            store(source).start()
 
     @pl.when(stage == pipes - 1)
     def _():
-        zeros[...] = jnp.zeros_like(zeros)
-        move(zeros)
-
-    for copy in small:
-        copy.wait()
+        rows_ref[...] = jnp.zeros_like(rows_ref)
+        for source in range(n):
+            store(source).start()
+
+    short_out[...] = short_ref[...]
+    long_out[...] = long_ref[...]
+    for source in range(n):
+        store(source).wait()
 
 
 def body(n, pipes, section_input, out_grad, short_filter, long_filter):
@@ -347,16 +353,17 @@
     vmem = pl.BlockSpec(memory_space=pltpu.VMEM)
     anywhere = pl.BlockSpec(memory_space=pltpu.HBM)
     dma = pltpu.SemaphoreType.DMA
-    passed, short_grad, long_grad = pl.pallas_call(
+    parts, short_grad, long_grad = pl.pallas_call(
         functools.partial(kernel, n, pipes, chunks, tap_count, batch, factor),
         out_shape=(
-            jax.ShapeDtypeStruct((rows, channels), BF16),
+            jax.ShapeDtypeStruct((n, chunks, LANES, LANES), BF16),
             jax.ShapeDtypeStruct((tap_count, 2, width), F32),
             jax.ShapeDtypeStruct((2, groups, taps), F32),
         ),
         in_specs=[anywhere, anywhere, vmem, vmem],
         out_specs=(anywhere, vmem, vmem),
         scratch_shapes=[
+            pltpu.VMEM((2, chunks, n, LANES, LANES), BF16),
             pltpu.VMEM((2, chunks, n, LANES, LANES), BF16),
             pltpu.VMEM((2, per_chunk, n * PER_GROUP, LANES), BF16),
             pltpu.VMEM((per_chunk, n * PER_GROUP, LANES), BF16),
@@ -367,7 +374,7 @@
             pltpu.VMEM((2 * tap_count, LANES, LANES), F32),
             pltpu.VMEM((2 * groups * 8, LANES), F32),
             pltpu.VMEM((2, groups, LANES), F32),
-            pltpu.VMEM((tap_count * LANES, 2 * LANES), BF16),
+            dma((2, chunks, n)),
             dma((2, chunks, n)),
             dma((2, chunks, n)),
             dma((2, chunks)),
@@ -380,12 +387,16 @@
     )(section_input[0], out_grad[0], short_filter[0].transpose(1, 0, 2), long_filter[0])
     passed, short_grad, long_grad = pl.pallas_call(
         functools.partial(finish, pipes),
-        out_shape=tuple(jax.ShapeDtypeStruct(x.shape, x.dtype) for x in (passed, short_grad, long_grad)),
-        in_specs=[anywhere] * 3,
-        out_specs=(anywhere,) * 3,
-        scratch_shapes=[pltpu.VMEM((rows, channels), BF16), dma((8,)), dma(()), dma(())],
+        out_shape=(
+            jax.ShapeDtypeStruct((rows, channels), BF16),
+            jax.ShapeDtypeStruct(short_grad.shape, F32),
+            jax.ShapeDtypeStruct(long_grad.shape, F32),
+        ),
+        in_specs=[anywhere, vmem, vmem],
+        out_specs=(anywhere, vmem, vmem),
+        scratch_shapes=[pltpu.VMEM((rows, channels), BF16), dma((n, chunks)), dma((n,))],
         compiler_params=pltpu.CompilerParams(vmem_limit_bytes=63 * 1024 * 1024),
-    )(passed, short_grad, long_grad)
+    )(parts, short_grad, long_grad)
     return passed[None], short_grad.transpose(1, 0, 2)[None], long_grad[None]
 
 

time: 88.7 us -> 57.7 us (0.65)
  Pallas kernels: 87.6 us -> 56.7 us
    pallas_call x1, Pallas kernels: 34.8 us -> 3.58 us  [body(): pl.pallas_call(functools.partial(finish, pipes), out_shape=(jax.ShapeDtyp...]
where the time goes in v5:
time: 57.7 us; the launch traced here: 57.3 us
  Pallas kernels  56.7 us (98%)
  between operations  0.64 us (1%)
    pallas_call x1, Pallas kernels, body(): pl.pallas_call(functools.partial(kernel, n, pipes, chunks, tap_count, bat...  53.1 us
    pallas_call x1, Pallas kernels, body(): pl.pallas_call(functools.partial(finish, pipes), out_shape=(jax.ShapeDtyp...  3.58 us

profile of v5, /device:TPU:13, one launch (start us, length us, event | category | flops | bytes accessed | tf_op | source)
XLA Modules:
  0.0 57.3 jit_solution(10556111769917156160)
XLA Ops:
  0.6 53.1 %shard_map.67 = (bf16[8,4,128,128]{3,2,1,0:T(8,128)(2,1)}, f32[7,2,512]{2,1,0:T(2,128)}, f32[2,32,128]{2,1,0:T(8,128)}) custom-call(bf16[128,4096]{1,0:T(8,128)(2,1)} %bitcast.11, bf16[128,4096]{1,0:T(8,128)(2,1)} %bitcast.12, bf16[7,2,512]{2,1,0:T(2,128)(2,1)} %bitcast.14, bf16[2,32,128]{2,1,0:T(8,128)(2,1)} %bitcast.13), custom_call_target="tpu_custom_call" | custom-call | tf_op jit(solution)/shard_map/pallas_call | solution.py:356
  53.7 3.6 %shard_map.68 = (bf16[128,4096]{1,0:T(8,128)(2,1)}, f32[7,2,512]{2,1,0:T(2,128)}, f32[2,32,128]{2,1,0:T(8,128)}) custom-call(bf16[8,4,128,128]{3,2,1,0:T(8,128)(2,1)} %get-tuple-element.9.parts_ref, f32[7,2,512]{2,1,0:T(2,128)} %get-tuple-element.10.short_ref, f32[2,32,128]{2,1,0:T(8,128)} %get-tuple-element.11.long_ref), custom_call_target="tpu_custom_call" | custom-call | tf_op jit(solution)/shard_map/pallas_call | solution.py:388

commit v6 on v5

--- a/solution.py
+++ b/solution.py
@@ -112,7 +112,7 @@
     def out_copy(q, j, to, source):
         return pltpu.make_async_remote_copy(
             src_ref=obuf.at[q, to],
-            dst_ref=out_ref.at[source, q],
+            dst_ref=out_ref.at[:, columns(source, q)],
             send_sem=osend_sem.at[q, j],
             recv_sem=orecv_sem.at[q, j],
             device_id=(stage - 1, to),
@@ -172,6 +172,19 @@
             circ = pltpu.roll(jnp.broadcast_to(filt, square), 0, 1, stride=1, stride_axis=0)
             now_ref[blk, g] = jnp.where(upper, circ, 0.0).astype(BF16)
             past_ref[blk, g] = jnp.where(upper, 0.0, circ).astype(BF16)
+
+    hold = min(1, chunks - 1)
+
+    def arrive(q):
+        for j in range(1, n):
+            for a in range(2):
+                in_copy(a, q, j, flip(me, j), flip(me, j)).wait_recv()
+        for a in range(2):
+            own_copy(a, q).wait()
+
+    def send_far(q):
+        for step in orders(n)[:-1]:
+            out_copy(q, *pick(step), me).start()
 
     def causal(v, blk, g):
         return mm(
@@ -216,11 +229,10 @@
 
     @pl.loop(0, chunks)
     def _(q):
-        for j in range(1, n):
-            for a in range(2):
-                in_copy(a, q, j, flip(me, j), flip(me, j)).wait_recv()
-        for a in range(2):
-            own_copy(a, q).wait()
+        @pl.when(q <= hold)
+        def _():
+            arrive(q)
+
         for a in range(2):
             for b in range(n):
                 turned = mm(eye, recv[a, q, b], NT).astype(BF16)
@@ -256,8 +268,22 @@
             for b in range(n):
                 piece = ot[:, b * PER_GROUP:(b + 1) * PER_GROUP, :].reshape(square)
                 obuf[q, b] = mm(eye, piece, NT).astype(BF16)
-            for step in orders(n) + [(0, 0)]:
-                out_copy(q, *pick(step), me).start()
+            for j in range(2):
+                out_copy(q, j, flip(me, j), me).start()
+
+        @pl.when(q == hold)
+        def _():
+            for later in range(hold + 1, chunks):
+                arrive(later)
+
+            @pl.when(stage > 0)
+            def _():
+                for earlier in range(hold + 1):
+                    send_far(earlier)
+
+        @pl.when((q > hold) & (stage > 0))
+        def _():
+            send_far(q)
 
         ones = jnp.ones((8, 2 * LANES), BF16)
         for blk in range(2):
@@ -298,46 +324,53 @@
                 out_copy(q, j, flip(me, j), flip(me, j)).wait_recv()
 
 
-def finish(pipes, parts_ref, short_ref, long_ref, out_ref, short_out, long_out, rows_ref, in_sem, out_sem):
+def finish(pipes, passed_ref, short_ref, long_ref, out_ref, short_out, long_out,
+           rows_ref, short_buf, long_buf, in_sem, out_sem, small_sem):
     stage = lax.axis_index("pipe")
-    n, chunks = parts_ref.shape[:2]
-    width = chunks * LANES
-
-    def columns(source):
-        return pl.ds(source * width, width)
-
-    def load(source, q):
-        return pltpu.make_async_copy(
-            parts_ref.at[source, q],
-            rows_ref.at[:, pl.ds(source * width + q * LANES, LANES)],
-            in_sem.at[source, q],
-        )
-
-    def store(source):
-        return pltpu.make_async_copy(
-            rows_ref.at[:, columns(source)], out_ref.at[:, columns(source)], out_sem.at[source]
-        )
+    parts = in_sem.shape[0]
+    size = passed_ref.shape[0] // parts
+
+    def piece(i):
+        return pl.ds(i * size, size)
+
+    def load(i):
+        return pltpu.make_async_copy(passed_ref.at[piece(i)], rows_ref.at[piece(i)], in_sem.at[i])
+
+    def store(i):
+        return pltpu.make_async_copy(rows_ref.at[piece(i)], out_ref.at[piece(i)], out_sem.at[i])
+
+    small_in = [
+        pltpu.make_async_copy(short_ref, short_buf, small_sem.at[0]),
+        pltpu.make_async_copy(long_ref, long_buf, small_sem.at[1]),
+    ]
+    small_out = [
+        pltpu.make_async_copy(short_buf, short_out, small_sem.at[2]),
+        pltpu.make_async_copy(long_buf, long_out, small_sem.at[3]),
+    ]
+    for copy in small_in:
+        copy.start()
 
     @pl.when(stage < pipes - 1)
     def _():
-        for source in range(n):
-            for q in range(chunks):
-                load(source, q).start()
-        for source in range(n):
-            for q in range(chunks):
-                load(source, q).wait()
-            store(source).start()
+        for i in range(parts):
+            load(i).start()
+        for i in range(parts):
+            load(i).wait()
+            store(i).start()
 
     @pl.when(stage == pipes - 1)
     def _():
         rows_ref[...] = jnp.zeros_like(rows_ref)
-        for source in range(n):
-            store(source).start()
-
-    short_out[...] = short_ref[...]
-    long_out[...] = long_ref[...]
-    for source in range(n):
-        store(source).wait()
+        for i in range(parts):
+            store(i).start()
+
+    for arrived, leaving in zip(small_in, small_out):
+        arrived.wait()
+        leaving.start()
+    for copy in small_out:
+        copy.wait()
+    for i in range(parts):
+        store(i).wait()
 
 
 def body(n, pipes, section_input, out_grad, short_filter, long_filter):
@@ -356,7 +389,7 @@
     parts, short_grad, long_grad = pl.pallas_call(
         functools.partial(kernel, n, pipes, chunks, tap_count, batch, factor),
         out_shape=(
-            jax.ShapeDtypeStruct((n, chunks, LANES, LANES), BF16),
+            jax.ShapeDtypeStruct((rows, channels), BF16),
             jax.ShapeDtypeStruct((tap_count, 2, width), F32),
             jax.ShapeDtypeStruct((2, groups, taps), F32),
         ),
@@ -392,9 +425,16 @@
             jax.ShapeDtypeStruct(short_grad.shape, F32),
             jax.ShapeDtypeStruct(long_grad.shape, F32),
         ),
-        in_specs=[anywhere, vmem, vmem],
-        out_specs=(anywhere, vmem, vmem),
-        scratch_shapes=[pltpu.VMEM((rows, channels), BF16), dma((n, chunks)), dma((n,))],
+        in_specs=[anywhere] * 3,
+        out_specs=(anywhere,) * 3,
+        scratch_shapes=[
+            pltpu.VMEM((rows, channels), BF16),
+            pltpu.VMEM(short_grad.shape, F32),
+            pltpu.VMEM(long_grad.shape, F32),
+            dma((8,)),
+            dma((8,)),
+            dma((4,)),
+        ],
         compiler_params=pltpu.CompilerParams(vmem_limit_bytes=63 * 1024 * 1024),
     )(parts, short_grad, long_grad)
     return passed[None], short_grad.transpose(1, 0, 2)[None], long_grad[None]

time: 57.7 us -> 58.2 us (level)
  the two profiles are of different devices: /device:TPU:13 before, /device:TPU:0 now
where the time goes in v6:
time: 58.2 us; the launch traced here: 57.8 us
  Pallas kernels  57.2 us (98%)
  between operations  0.64 us (1%)
    pallas_call x1, Pallas kernels, body(): pl.pallas_call(functools.partial(kernel, n, pipes, chunks, tap_count, bat...  55 us
    pallas_call x1, Pallas kernels, body(): pl.pallas_call(functools.partial(finish, pipes), out_shape=(jax.ShapeDtyp...  2.17 us

profile of v6, /device:TPU:0, one launch (start us, length us, event | category | flops | bytes accessed | tf_op | source)
XLA Modules:
  0.0 57.8 jit_solution(7157156076307564930)
XLA Ops:
  0.6 55.0 %shard_map.67 = (bf16[128,4096]{1,0:T(8,128)(2,1)}, f32[7,2,512]{2,1,0:T(2,128)}, f32[2,32,128]{2,1,0:T(8,128)}) custom-call(bf16[128,4096]{1,0:T(8,128)(2,1)} %bitcast.11, bf16[128,4096]{1,0:T(8,128)(2,1)} %bitcast.12, bf16[7,2,512]{2,1,0:T(2,128)(2,1)} %bitcast.14, bf16[2,32,128]{2,1,0:T(8,128)(2,1)} %bitcast.13), custom_call_target="tpu_custom_call" | custom-call | tf_op jit(solution)/shard_map/pallas_call | solution.py:389
  55.6 2.2 %shard_map.68 = (bf16[128,4096]{1,0:T(8,128)(2,1)}, f32[7,2,512]{2,1,0:T(2,128)}, f32[2,32,128]{2,1,0:T(8,128)}) custom-call(bf16[128,4096]{1,0:T(8,128)(2,1)} %get-tuple-element.9.passed_ref, f32[7,2,512]{2,1,0:T(2,128)} %get-tuple-element.10.short_ref, f32[2,32,128]{2,1,0:T(8,128)} %get-tuple-element.11.long_ref), custom_call_target="tpu_custom_call" | custom-call | tf_op jit(solution)/shard_map/pallas_call | solution.py:421

commit v7 on v3

--- a/solution.py
+++ b/solution.py
@@ -307,6 +307,55 @@
         def _(q):
             for j in range(n):
                 out_copy(q, j, flip(me, j), flip(me, j)).wait_recv()
+
+
+def finish(pipes, passed_ref, short_ref, long_ref, out_ref, short_out, long_out,
+           rows_ref, short_buf, long_buf, in_sem, out_sem, small_sem):
+    stage = lax.axis_index("pipe")
+    parts = in_sem.shape[0]
+    size = passed_ref.shape[0] // parts
+
+    def piece(i):
+        return pl.ds(i * size, size)
+
+    def load(i):
+        return pltpu.make_async_copy(passed_ref.at[piece(i)], rows_ref.at[piece(i)], in_sem.at[i])
+
+    def store(i):
+        return pltpu.make_async_copy(rows_ref.at[piece(i)], out_ref.at[piece(i)], out_sem.at[i])
+
+    small_in = [
+        pltpu.make_async_copy(short_ref, short_buf, small_sem.at[0]),
+        pltpu.make_async_copy(long_ref, long_buf, small_sem.at[1]),
+    ]
+    small_out = [
+        pltpu.make_async_copy(short_buf, short_out, small_sem.at[2]),
+        pltpu.make_async_copy(long_buf, long_out, small_sem.at[3]),
+    ]
+    for copy in small_in:
+        copy.start()
+
+    @pl.when(stage < pipes - 1)
+    def _():
+        for i in range(parts):
+            load(i).start()
+        for i in range(parts):
+            load(i).wait()
+            store(i).start()
+
+    @pl.when(stage == pipes - 1)
+    def _():
+        rows_ref[...] = jnp.zeros_like(rows_ref)
+        for i in range(parts):
+            store(i).start()
+
+    for arrived, leaving in zip(small_in, small_out):
+        arrived.wait()
+        leaving.start()
+    for copy in small_out:
+        copy.wait()
+    for i in range(parts):
+        store(i).wait()
 
 
 def body(n, pipes, section_input, out_grad, short_filter, long_filter):
@@ -354,7 +403,25 @@
             collective_id=0, has_side_effects=True, vmem_limit_bytes=63 * 1024 * 1024
         ),
     )(section_input[0], out_grad[0], short_filter[0].transpose(1, 0, 2), long_filter[0])
-    passed = jnp.where(lax.axis_index("pipe") < pipes - 1, passed, jnp.zeros_like(passed))
+    passed, short_grad, long_grad = pl.pallas_call(
+        functools.partial(finish, pipes),
+        out_shape=(
+            jax.ShapeDtypeStruct((rows, channels), BF16),
+            jax.ShapeDtypeStruct(short_grad.shape, F32),
+            jax.ShapeDtypeStruct(long_grad.shape, F32),
+        ),
+        in_specs=[anywhere] * 3,
+        out_specs=(anywhere,) * 3,
+        scratch_shapes=[
+            pltpu.VMEM((rows, channels), BF16),
+            pltpu.VMEM(short_grad.shape, F32),
+            pltpu.VMEM(long_grad.shape, F32),
+            dma((8,)),
+            dma((8,)),
+            dma((4,)),
+        ],
+        compiler_params=pltpu.CompilerParams(vmem_limit_bytes=63 * 1024 * 1024),
+    )(passed, short_grad, long_grad)
     return passed[None], short_grad.transpose(1, 0, 2)[None], long_grad[None]
 
 

time: 56.4 us -> 54.9 us (0.973)
  other arithmetic: 2.28 us -> 0 us
  Pallas kernels: 51.7 us -> 53.9 us
  local copies, waits for them, and re-layouts: 1.38 us -> 0 us
    broadcast_in_dim x1 -> x0, other arithmetic: 2.28 us -> none  [body(): return (passed[None], short_grad.transpose(1, 0, 2)[None], long_grad[None])]
    pallas_call x0 -> x1, Pallas kernels: none -> 2.17 us  [body(): pl.pallas_call(functools.partial(finish, pipes), out_shape=(jax.ShapeDtyp...]
    unnamed x6 -> x0, local copies, waits for them, and re-layouts: 1.38 us -> none
where the time goes in v7:
time: 54.9 us; the launch traced here: 54.5 us
  Pallas kernels  53.9 us (98%)
  between operations  0.64 us (1%)
    pallas_call x1, Pallas kernels, body(): pl.pallas_call(functools.partial(kernel, n, pipes, chunks, tap_count, bat...  51.7 us
    pallas_call x1, Pallas kernels, body(): pl.pallas_call(functools.partial(finish, pipes), out_shape=(jax.ShapeDtyp...  2.17 us

profile of v7, /device:TPU:0, one launch (start us, length us, event | category | flops | bytes accessed | tf_op | source)
XLA Modules:
  0.0 54.5 jit_solution(16110636817458558082)
XLA Ops:
  0.6 51.7 %shard_map.67 = (bf16[128,4096]{1,0:T(8,128)(2,1)}, f32[7,2,512]{2,1,0:T(2,128)}, f32[2,32,128]{2,1,0:T(8,128)}) custom-call(bf16[128,4096]{1,0:T(8,128)(2,1)} %bitcast.11, bf16[128,4096]{1,0:T(8,128)(2,1)} %bitcast.12, bf16[7,2,512]{2,1,0:T(2,128)(2,1)} %bitcast.14, bf16[2,32,128]{2,1,0:T(8,128)(2,1)} %bitcast.13), custom_call_target="tpu_custom_call" | custom-call | tf_op jit(solution)/shard_map/pallas_call | solution.py:374
  52.4 2.2 %shard_map.68 = (bf16[128,4096]{1,0:T(8,128)(2,1)}, f32[7,2,512]{2,1,0:T(2,128)}, f32[2,32,128]{2,1,0:T(8,128)}) custom-call(bf16[128,4096]{1,0:T(8,128)(2,1)} %get-tuple-element.9.passed_ref, f32[7,2,512]{2,1,0:T(2,128)} %get-tuple-element.10.short_ref, f32[2,32,128]{2,1,0:T(8,128)} %get-tuple-element.11.long_ref), custom_call_target="tpu_custom_call" | custom-call | tf_op jit(solution)/shard_map/pallas_call | solution.py:406
